TPU v7x, 128 devices: a whole 4x4x4 slice. The times are simulated.
128 devices in a mesh: segment: 4 (over x_lo, core), space: 32 (over y, x_hi, z).
Axes of the slice: x: 4 (x_hi: 2, x_lo: 2; x = x_hi * 2 + x_lo), y: 4, z: 4, core: 2. Of those that a mesh axis runs over, the one named last changes fastest.
Arguments:
- state: float32 [2, 5, 2, 256, 64], P(None, None, None, 'space'), may hold values from -6 to 6
- noise: float32 [2, 4, 2, 256, 64], P(None, None, None, 'space'), may hold values from -6 to 6
- land_sea: int32 [256, 64], P('space'), may hold values 0 or 1
- observed_truth: float32 [2, 5, 2, 256, 64], P(None, None, None, 'space', 'segment'), may hold values from -6 to 6
- embed_w: float32 [7, 256], replicated, may hold values from -2 to 2
- fine_weight_kernels: bfloat16 [2, 6912, 128], replicated, may hold values from -0.078125 to 0.078125
- merge_w: bfloat16 [512, 256], replicated, may hold values from -0.25 to 0.25
- coarse_w: bfloat16 [4, 6912, 256], replicated, may hold values from -0.078125 to 0.078125
- expand_w: bfloat16 [256, 512], replicated, may hold values from -0.375 to 0.375
- head_w: bfloat16 [128, 5], replicated, may hold values from -0.5 to 0.5
Outputs:
- member_prediction: float32 [2, 4, 5, 2, 256, 64], P(None, None, None, None, 'space', 'segment')
- crps: float32 [2, 5, 2, 256, 64], P(None, None, None, 'space', 'segment')
All inputs are finite; a program needn't handle non-finite values. No bound on the sum of `land_sea` on one device may be relied on, other than what follows from the above.
Results may differ from a plain program's by a relative error of at most 0.0022.
Values may be sent and summed in bfloat16 or wider, within the bound.
No kernel may reach another device: no remote copies, remote signals or barrier semaphores. Data moves between devices by JAX's collectives and lax.ppermute only.
A program may use at most 192 MiB of HBM per device.

v0:
```python
import jax
import jax.numpy as jnp
from jax import lax
from jax.sharding import PartitionSpec as P


def extended(block, sides, width):
    for axis, dim in sides:
        count = lax.axis_size(axis)
        forward = [(i, i + 1) for i in range(count - 1)]
        backward = [(target, source) for source, target in forward]
        low = lax.ppermute(
            lax.slice_in_dim(block, block.shape[dim] - width, None, axis=dim), axis, forward
        )
        high = lax.ppermute(lax.slice_in_dim(block, 0, width, axis=dim), axis, backward)
        block = jnp.concatenate([low, block, high], axis=dim)
    return block


def from_behind(value, axis, by):
    peers = lax.axis_size(axis)
    pairs = [(i, i + by) for i in range(peers) if 0 <= i + by < peers]
    return lax.ppermute(value, axis, pairs)


def conv_member(padded, weight):
    span_z = padded.shape[0] - 2
    span_y = padded.shape[1] - 2
    span_x = padded.shape[2] - 2
    taps = [
        padded[depth : depth + span_z, north : north + span_y, east : east + span_x, :]
        for depth in range(3)
        for north in range(3)
        for east in range(3)
    ]
    stacked = jnp.concatenate(taps, axis=-1)
    flat = stacked.reshape(span_z * span_y * span_x, stacked.shape[-1])
    result = jnp.dot(flat, weight, preferred_element_type=jnp.float32)
    return result.reshape(span_z, span_y, span_x, weight.shape[-1])


def conv_layer(haloed, weight):
    lon_pad = (1, 1)
    padded = jnp.pad(haloed, ((0, 0), (1, 1), (0, 0), lon_pad, (0, 0)))
    return lax.map(lambda member: conv_member(member, weight), padded)


def embed_fields(state_m, noise_m, land_sea, embed_w):
    members = noise_m.shape[0]
    moved = jnp.transpose(state_m, (1, 2, 3, 0))
    base = jnp.broadcast_to(moved[None], (members,) + moved.shape)
    land = jnp.broadcast_to(
        land_sea.astype(jnp.float32)[None, None, :, :, None], noise_m.shape + (1,)
    )
    feats = jnp.concatenate([base, noise_m[..., None], land], axis=-1)
    mixed = jnp.einsum("bzyxf,fc->bzyxc", feats, embed_w, precision=lax.Precision.HIGHEST)
    return jax.nn.gelu(mixed).astype(jnp.bfloat16)


def merge_patches(fine, merge_w):
    bsz, zsz, ysz, xsz, csz = fine.shape
    grouped = fine.reshape(bsz, zsz, ysz // 2, 2, xsz // 2, 2, csz).transpose(0, 1, 2, 4, 3, 5, 6)
    grouped = grouped.reshape(bsz, zsz, ysz // 2, xsz // 2, 4 * csz)
    return jax.nn.gelu(jnp.dot(grouped, merge_w, preferred_element_type=jnp.float32)).astype(
        jnp.bfloat16
    )


def expand_patches(coarse, expand_w):
    bsz, zsz, ysz, xsz, _ = coarse.shape
    narrow = expand_w.shape[1] // 4
    spread = jnp.dot(coarse, expand_w, preferred_element_type=jnp.float32).astype(jnp.bfloat16)
    spread = spread.reshape(bsz, zsz, ysz, xsz, 2, 2, narrow).transpose(0, 1, 2, 4, 3, 5, 6)
    return spread.reshape(bsz, zsz, 2 * ysz, 2 * xsz, narrow)


def residual_step(fields_in, conv_out):
    return (fields_in.astype(jnp.float32) + jax.nn.gelu(conv_out)).astype(jnp.bfloat16)


def fine_out(conv_out):
    return jax.nn.gelu(conv_out).astype(jnp.bfloat16)


def head_term(decoded, head_w):
    return jnp.transpose(
        jnp.dot(decoded, head_w, preferred_element_type=jnp.float32), (0, 4, 1, 2, 3)
    )


def probabilistic_skill_aggregate(pred, truth):
    members = pred.shape[0]
    skill = jnp.mean(jnp.abs(pred - truth[None]), axis=0)
    spread = jnp.sum(jnp.abs(pred[:, None] - pred[None, :]), axis=(0, 1)) / (
        2.0 * members * (members - 1)
    )
    return skill - spread


def fine_rim(fields_in):
    return extended(fields_in, (("space", 2),), 1)


def coarse_rim(fields_in):
    return extended(fields_in, (("space", 2),), 1)


def body(
    state,
    noise,
    land_sea,
    observed_truth,
    embed_w,
    fine_weight_kernels,
    merge_w,
    coarse_w,
    expand_w,
    head_w,
):
    segments = lax.axis_size("segment")
    section = lax.axis_index("segment")
    small_batch_slice = state.shape[0]
    fields = state.shape[1]
    levels = state.shape[2]
    lat_rows = state.shape[3]
    lon_cols = state.shape[4]
    members = noise.shape[1]
    narrow = fine_weight_kernels.shape[2]
    broad = coarse_w.shape[2]
    lon_part = lon_cols // segments
    first_col = section * lon_part
    atmosphere_share = lax.dynamic_slice_in_dim(state, first_col, lon_part, 4)
    fine_zero = jnp.zeros((members, levels, lat_rows, lon_cols, narrow), jnp.bfloat16)
    received = jnp.zeros((members, levels, lat_rows // 2, lon_cols // 2, broad), jnp.bfloat16)
    increments = jnp.zeros(
        (small_batch_slice, members, fields, levels, lat_rows, lon_cols), jnp.float32
    )
    held = jnp.zeros((small_batch_slice, members, levels, lat_rows, lon_cols, narrow), jnp.bfloat16)
    head_zero = jnp.zeros((members, fields, levels, lat_rows, lon_cols), jnp.float32)
    for moment in range(small_batch_slice + segments - 1):
        offset = moment - section
        active = (offset >= 0) & (offset < small_batch_slice)
        slot = jnp.clip(offset, 0, small_batch_slice - 1)
        first_segment = active & (section == 0)
        second_segment = active & (section == 1)
        third_segment = active & (section == 2)
        last_segment = active & (section == segments - 1)
        state_now = lax.dynamic_index_in_dim(state, slot, 0, False)
        noise_now = lax.dynamic_index_in_dim(noise, slot, 0, False)
        embedded = embed_fields(state_now, noise_now, land_sea, embed_w)
        if 0 <= moment - segments + 1 < small_batch_slice:
            skip_now = from_behind(held[moment - segments + 1], "segment", segments - 1)
        else:
            skip_now = fine_zero
        combined_tensor = lax.cond(
            last_segment,
            lambda: jnp.concatenate([expand_patches(received, expand_w), skip_now], axis=-1),
            lambda: embedded,
        )
        joined_rim = fine_rim(combined_tensor)
        chosen = lax.dynamic_index_in_dim(
            fine_weight_kernels, jnp.where(last_segment, 1, 0), 0, False
        )
        first = lax.cond(
            first_segment | last_segment,
            lambda: fine_out(conv_layer(joined_rim, chosen)),
            lambda: fine_zero,
        )
        last = first
        if moment < small_batch_slice:
            held = held.at[moment].set(first)
        coarse_in = lax.cond(first_segment, lambda: merge_patches(first, merge_w), lambda: received)
        coarse_rim_in = coarse_rim(coarse_in)
        layer_pick = jnp.where(section == 0, 0, jnp.where(section == 1, 1, 3))
        coarse_weight = lax.dynamic_index_in_dim(coarse_w, layer_pick, 0, False)
        coarse_mid = lax.cond(
            first_segment | second_segment | third_segment,
            lambda: residual_step(coarse_in, conv_layer(coarse_rim_in, coarse_weight)),
            lambda: coarse_in,
        )
        coarse_rim_mid = coarse_rim(coarse_mid)
        coarse_out = lax.cond(
            second_segment,
            lambda: residual_step(coarse_mid, conv_layer(coarse_rim_mid, coarse_w[2])),
            lambda: coarse_mid,
        )
        head_now = lax.cond(last_segment, lambda: head_term(last, head_w), lambda: head_zero)
        increments = jnp.where(
            last_segment, lax.dynamic_update_index_in_dim(increments, head_now, slot, 0), increments
        )
        received = from_behind(coarse_out, "segment", 1)
    passed_along = lax.psum_scatter(
        increments.astype(jnp.bfloat16), "segment", scatter_dimension=5, tiled=True
    ).astype(jnp.float32)
    member_prediction = atmosphere_share[:, None] + passed_along
    skill_entries = jnp.stack(
        [
            probabilistic_skill_aggregate(
                member_prediction[sample_count], observed_truth[sample_count]
            )
            for sample_count in range(small_batch_slice)
        ]
    )
    return (member_prediction, skill_entries)


def solution(mesh):
    return jax.shard_map(
        body,
        mesh=mesh,
        in_specs=(
            P(None, None, None, "space", None),
            P(None, None, None, "space", None),
            P("space", None),
            P(None, None, None, "space", "segment"),
            P(),
            P(),
            P(),
            P(),
            P(),
            P(),
        ),
        out_specs=(
            P(None, None, None, None, "space", "segment"),
            P(None, None, None, "space", "segment"),
        ),
        check_vma=False,
    )
```

profile of v0, /device:TPU:17, one launch (start us, length us, event | category | flops | bytes accessed | tf_op | source)
XLA Modules:
  0.0 638.4 jit_solution(10402847724106640329)
XLA Ops:
  18.8 8.0 %collective-permute-start.1 = (bf16[4,2,1,64,256]{4,3,2,1,0:T(8,128)(2,1)}, bf16[4,2,1,64,256]{4,3,2,1,0:T(8,128)(2,1)}, u32[]{:S(2)}, u32[]{:S(2)}) collective-permute-start(bf16[4,2,1,64,256]{4,3,2,1,0:T(8,128)(2,1)} %get-tuple-element.824), channel_id=1, source_target_pairs={{1,0},{2,1},{3,2},{4,3},{5,4},{6,5},{7,6},{8,7},{9,8},{10,9},{11,1... | collective-permute-start | bytes 786440 | tf_op jit(solution)/shard_map/ppermute | solution.py:15
  32.0 8.3 %collective-permute-done = bf16[4,2,1,64,256]{4,3,2,1,0:T(8,128)(2,1)} collective-permute-done((bf16[4,2,1,64,256]{4,3,2,1,0:T(8,128)(2,1)}, bf16[4,2,1,64,256]{4,3,2,1,0:T(8,128)(2,1)}, u32[]{:S(2)}, u32[]{:S(2)}) %collective-permute-start) | collective-permute-done | bytes 262176 | tf_op jit(solution)/shard_map/ppermute | solution.py:12
  70.4 7.9 %collective-permute-done.4 = bf16[4,2,1,32,256]{4,3,2,1,0:T(8,128)(2,1)} collective-permute-done((bf16[4,2,1,32,256]{4,3,2,1,0:T(8,128)(2,1)}, bf16[4,2,1,32,256]{4,3,2,1,0:T(8,128)(2,1)}, u32[]{:S(2)}, u32[]{:S(2)}) %collective-permute-start.4) | collective-permute-done | bytes 131104 | tf_op jit(solution)/shard_map/ppermute | solution.py:12
  87.1 6.5 %fusion.279 = bf16[4,2,8,64,256]{4,3,2,1,0:T(8,128)(2,1)} fusion(f32[4,2,8,64,1]{3,4,2,1,0:T(1,128)} %copy-done.20, f32[4,2,8,64,1]{3,4,2,1,0:T(1,128)} %bitcast.544, f32[4,2,8,64,5]{3,4,2,1,0:T(8,128)S(1)} %broadcast_in_dim.156, f32[7,256]{1,0:T(8,128)S(1)} %copy-done), kind=kOutput, calls=%fused_computation.634 | convolution fusion | flops 97574912 | bytes 2219008 | tf_op jit(solution)/shard_map/bzyxf,fc->bzyxc/dot_general | solution.py:56
  93.5 76.3 %collective-permute-done.6 = bf16[4,2,4,32,256]{4,3,2,1,0:T(8,128)(2,1)} collective-permute-done((bf16[4,2,4,32,256]{4,3,2,1,0:T(8,128)(2,1)}, bf16[4,2,4,32,256]{4,3,2,1,0:T(8,128)(2,1)}, u32[]{:S(2)}, u32[]{:S(2)}) %collective-permute-start.6) | collective-permute-done | bytes 524320 | tf_op jit(solution)/shard_map/ppermute | solution.py:23
  179.6 6.4 %collective-permute-done.7 = bf16[4,2,1,64,256]{4,3,2,1,0:T(8,128)(2,1)} collective-permute-done((bf16[4,2,1,64,256]{4,3,2,1,0:T(8,128)(2,1)}, bf16[4,2,1,64,256]{4,3,2,1,0:T(8,128)(2,1)}, u32[]{:S(2)}, u32[]{:S(2)}) %collective-permute-start.7) | collective-permute-done | bytes 262176 | tf_op jit(solution)/shard_map/ppermute | solution.py:12
  200.0 6.4 %collective-permute-done.9 = bf16[4,2,1,32,256]{4,3,2,1,0:T(8,128)(2,1)} collective-permute-done((bf16[4,2,1,32,256]{4,3,2,1,0:T(8,128)(2,1)}, bf16[4,2,1,32,256]{4,3,2,1,0:T(8,128)(2,1)}, u32[]{:S(2)}, u32[]{:S(2)}) %collective-permute-start.9) | collective-permute-done | bytes 131104 | tf_op jit(solution)/shard_map/ppermute | solution.py:12
  208.6 24.9 %conditional.37 = (bf16[4,2,4,32,256]{4,3,2,1,0:T(8,128)(2,1)}) conditional(s32[]{:T(128)} %convert_element_type.238, bf16[4,2,4,32,256]{4,3,2,1,0:T(8,128)(2,1)} %get-tuple-element.1397, (bf16[4,2,4,32,256]{4,3,2,1,0:T(8,128)(2,1)}, bf16[4,2,6,32,256]{4,3,2,1,0:T(8,128)(2,1)}, bf16[6912,256]{1,0:T(8,128)(2,1)}) %tuple.270), branch_computations={%region_28.29_spmd, %region_29.32_spmd} | conditional | flops 908853248 | bytes 33964192 | solution.py:176
  211.5 19.5 %while.137 = (s32[]{:T(128)}, f32[4,2,4,32,256]{4,3,2,1,0:T(8,128)}, bf16[4,4,6,34,256]{4,3,2,1,0:T(8,128)(2,1)}, bf16[6912,256]{1,0:T(8,128)(2,1)}, s32[]{:T(128)}) while((s32[]{:T(128)}, f32[4,2,4,32,256]{4,3,2,1,0:T(8,128)}, bf16[4,4,6,34,256]{4,3,2,1,0:T(8,128)(2,1)}, bf16[6912,256]{1,0:T(8,128)(2,1)}, s32[]{:T(128)}) %tuple.455), condition=%wide.region_31.31_spmd, body=%wide.region_30.30_spmd.sunk | while | flops 905969664 | bytes 29409384 | solution.py:45
  241.2 6.4 %collective-permute-done.11 = bf16[4,2,1,32,256]{4,3,2,1,0:T(8,128)(2,1)} collective-permute-done((bf16[4,2,1,32,256]{4,3,2,1,0:T(8,128)(2,1)}, bf16[4,2,1,32,256]{4,3,2,1,0:T(8,128)(2,1)}, u32[]{:S(2)}, u32[]{:S(2)}) %collective-permute-start.11) | collective-permute-done | bytes 131104 | tf_op jit(solution)/shard_map/ppermute | solution.py:12
  249.8 29.0 %conditional.38 = (bf16[4,2,4,32,256]{4,3,2,1,0:T(8,128)(2,1)}) conditional(s32[]{:T(128)} %convert_element_type.237, bf16[4,2,4,32,256]{4,3,2,1,0:T(8,128)(2,1)} %get-tuple-element.1398, (bf16[4,2,4,32,256]{4,3,2,1,0:T(8,128)(2,1)}, bf16[4,2,6,32,256]{4,3,2,1,0:T(8,128)(2,1)}, bf16[4,6912,256]{2,1,0:T(8,128)(2,1)}) %tuple.271), branch_computations={%region_32.33_spmd, %region_33.36_spmd} | conditional | flops 908853248 | bytes 41042080 | solution.py:182
  256.8 19.4 %while.138 = (s32[]{:T(128)}, f32[4,2,4,32,256]{4,3,2,1,0:T(8,128)}, bf16[4,4,6,34,256]{4,3,2,1,0:T(8,128)(2,1)}, bf16[6912,256]{1,0:T(8,128)(2,1)}, s32[]{:T(128)}) while((s32[]{:T(128)}, f32[4,2,4,32,256]{4,3,2,1,0:T(8,128)}, bf16[4,4,6,34,256]{4,3,2,1,0:T(8,128)(2,1)}, bf16[6912,256]{1,0:T(8,128)(2,1)}, s32[]{:T(128)}) %tuple.452), condition=%wide.region_35.35_spmd, body=%wide.region_34.34_spmd.sunk | while | flops 905969664 | bytes 29409384 | solution.py:45
  281.5 6.5 %fusion.287 = bf16[4,2,8,64,256]{4,3,2,1,0:T(8,128)(2,1)} fusion(f32[4,2,8,64,1]{3,4,2,1,0:T(1,128)} %copy-done.20, f32[4,2,8,64,1]{3,4,2,1,0:T(1,128)} %bitcast.543, f32[4,2,8,64,5]{3,4,2,1,0:T(8,128)S(1)} %broadcast_in_dim.158, f32[7,256]{1,0:T(8,128)S(1)} %copy-done), kind=kOutput, calls=%fused_computation.642 | convolution fusion | flops 97574912 | bytes 2219008 | tf_op jit(solution)/shard_map/bzyxf,fc->bzyxc/dot_general | solution.py:56
  288.0 33.8 %collective-permute-done.13 = bf16[4,2,4,32,256]{4,3,2,1,0:T(8,128)(2,1)} collective-permute-done((bf16[4,2,4,32,256]{4,3,2,1,0:T(8,128)(2,1)}, bf16[4,2,4,32,256]{4,3,2,1,0:T(8,128)(2,1)}, u32[]{:S(2)}, u32[]{:S(2)}) %collective-permute-start.13) | collective-permute-done | bytes 524320 | tf_op jit(solution)/shard_map/ppermute | solution.py:23
  331.2 6.4 %collective-permute-done.14 = bf16[4,2,1,64,256]{4,3,2,1,0:T(8,128)(2,1)} collective-permute-done((bf16[4,2,1,64,256]{4,3,2,1,0:T(8,128)(2,1)}, bf16[4,2,1,64,256]{4,3,2,1,0:T(8,128)(2,1)}, u32[]{:S(2)}, u32[]{:S(2)}) %collective-permute-start.14) | collective-permute-done | bytes 262176 | tf_op jit(solution)/shard_map/ppermute | solution.py:12
  358.9 25.3 %conditional.43 = (bf16[4,2,4,32,256]{4,3,2,1,0:T(8,128)(2,1)}) conditional(s32[]{:T(128)} %convert_element_type.244, bf16[4,2,4,32,256]{4,3,2,1,0:T(8,128)(2,1)} %get-tuple-element.1402, (bf16[4,2,4,32,256]{4,3,2,1,0:T(8,128)(2,1)}, bf16[4,2,6,32,256]{4,3,2,1,0:T(8,128)(2,1)}, bf16[6912,256]{1,0:T(8,128)(2,1)}) %tuple.278), branch_computations={%region_46.47_spmd, %region_47.50_spmd} | conditional | flops 908853248 | bytes 33964192 | solution.py:176
  362.2 19.5 %while.140 = (s32[]{:T(128)}, f32[4,2,4,32,256]{4,3,2,1,0:T(8,128)}, bf16[4,4,6,34,256]{4,3,2,1,0:T(8,128)(2,1)}, bf16[6912,256]{1,0:T(8,128)(2,1)}, s32[]{:T(128)}) while((s32[]{:T(128)}, f32[4,2,4,32,256]{4,3,2,1,0:T(8,128)}, bf16[4,4,6,34,256]{4,3,2,1,0:T(8,128)(2,1)}, bf16[6912,256]{1,0:T(8,128)(2,1)}, s32[]{:T(128)}) %tuple.446), condition=%wide.region_49.49_spmd, body=%wide.region_48.48_spmd.sunk | while | flops 905969664 | bytes 29409384 | solution.py:45
  391.9 6.4 %collective-permute-done.18 = bf16[4,2,1,32,256]{4,3,2,1,0:T(8,128)(2,1)} collective-permute-done((bf16[4,2,1,32,256]{4,3,2,1,0:T(8,128)(2,1)}, bf16[4,2,1,32,256]{4,3,2,1,0:T(8,128)(2,1)}, u32[]{:S(2)}, u32[]{:S(2)}) %collective-permute-start.18) | collective-permute-done | bytes 131104 | tf_op jit(solution)/shard_map/ppermute | solution.py:12
  400.5 29.0 %conditional.44 = (bf16[4,2,4,32,256]{4,3,2,1,0:T(8,128)(2,1)}) conditional(s32[]{:T(128)} %convert_element_type.243, bf16[4,2,4,32,256]{4,3,2,1,0:T(8,128)(2,1)} %get-tuple-element.1403, (bf16[4,2,4,32,256]{4,3,2,1,0:T(8,128)(2,1)}, bf16[4,2,6,32,256]{4,3,2,1,0:T(8,128)(2,1)}, bf16[4,6912,256]{2,1,0:T(8,128)(2,1)}) %tuple.279), branch_computations={%region_50.51_spmd, %region_51.54_spmd} | conditional | flops 908853248 | bytes 41042080 | solution.py:182
  407.5 19.5 %while.141 = (s32[]{:T(128)}, f32[4,2,4,32,256]{4,3,2,1,0:T(8,128)}, bf16[4,4,6,34,256]{4,3,2,1,0:T(8,128)(2,1)}, bf16[6912,256]{1,0:T(8,128)(2,1)}, s32[]{:T(128)}) while((s32[]{:T(128)}, f32[4,2,4,32,256]{4,3,2,1,0:T(8,128)}, bf16[4,4,6,34,256]{4,3,2,1,0:T(8,128)(2,1)}, bf16[6912,256]{1,0:T(8,128)(2,1)}, s32[]{:T(128)}) %tuple.443), condition=%wide.region_53.53_spmd, body=%wide.region_52.52_spmd.sunk | while | flops 905969664 | bytes 29409384 | solution.py:45
  432.3 6.5 %fusion.295 = bf16[4,2,8,64,256]{4,3,2,1,0:T(8,128)(2,1)} fusion(f32[4,2,8,64,1]{3,4,2,1,0:T(1,128)} %copy-done.20, f32[4,2,8,64,1]{3,4,2,1,0:T(1,128)} %bitcast.542, f32[4,2,8,64,5]{3,4,2,1,0:T(8,128)S(1)} %broadcast_in_dim.160, f32[7,256]{1,0:T(8,128)S(1)} %copy-done), kind=kOutput, calls=%fused_computation.650 | convolution fusion | flops 97574912 | bytes 2219008 | tf_op jit(solution)/shard_map/bzyxf,fc->bzyxc/dot_general | solution.py:56
  493.5 31.0 %collective-permute-start.28 = (bf16[4,2,4,32,256]{4,3,2,1,0:T(8,128)(2,1)}, bf16[4,2,4,32,256]{4,3,2,1,0:T(8,128)(2,1)}, u32[]{:S(2)}, u32[]{:S(2)}) collective-permute-start(bf16[4,2,4,32,256]{4,3,2,1,0:T(8,128)(2,1)} %get-tuple-element.1409), channel_id=1, source_target_pairs={{0,32},{32,64},{64,96},{1,33},{33,65},{65,97},{2,34},{34,66},{66,9... | collective-permute-start | bytes 1572872 | tf_op jit(solution)/shard_map/ppermute | solution.py:23
  525.4 6.5 %fusion.303 = bf16[4,2,8,64,256]{4,3,2,1,0:T(8,128)(2,1)} fusion(f32[4,2,8,64,1]{3,4,2,1,0:T(1,128)} %copy-done.20, f32[4,2,8,64,1]{3,4,2,1,0:T(1,128)} %bitcast.541, f32[4,2,8,64,5]{3,4,2,1,0:T(8,128)S(1)} %broadcast_in_dim.162, f32[7,256]{1,0:T(8,128)S(1)} %copy-done), kind=kOutput, calls=%fused_computation.658 | convolution fusion | flops 97574912 | bytes 2219008 | tf_op jit(solution)/shard_map/bzyxf,fc->bzyxc/dot_general | solution.py:56
  561.5 67.4 %reduce-scatter.4.cloned.1.call-done = bf16[16,640]{1,0:T(8,128)(2,1)} async-done(((bf16[64,640]{1,0:T(8,128)(2,1)}), bf16[16,640]{1,0:T(8,128)(2,1)}) %reduce-scatter.4.cloned.1.call-update) | async-done | bytes 20496
  (675 shorter events, 336.7 us)
Async XLA Ops:
  7.2 621.7 %reduce-scatter.4.cloned.1.call-start = ((), (), s32[]{:S(2)}) async-start(), calls=%async_computation.1 | async-start | bytes 102400
  18.8 13.2 %collective-permute-start.1 = (bf16[4,2,1,64,256]{4,3,2,1,0:T(8,128)(2,1)}, bf16[4,2,1,64,256]{4,3,2,1,0:T(8,128)(2,1)}, u32[]{:S(2)}, u32[]{:S(2)}) collective-permute-start(bf16[4,2,1,64,256]{4,3,2,1,0:T(8,128)(2,1)} %get-tuple-element.824), channel_id=1, source_target_pairs={{1,0},{2,1},{3,2},{4,3},{5,4},{6,5},{7,6},{8,7},{9,8},{10,9},{11,1... | collective-permute-start | bytes 786440 | tf_op jit(solution)/shard_map/ppermute | solution.py:15
  26.8 13.5 %collective-permute-start = (bf16[4,2,1,64,256]{4,3,2,1,0:T(8,128)(2,1)}, bf16[4,2,1,64,256]{4,3,2,1,0:T(8,128)(2,1)}, u32[]{:S(2)}, u32[]{:S(2)}) collective-permute-start(bf16[4,2,1,64,256]{4,3,2,1,0:T(8,128)(2,1)} %get-tuple-element.823), channel_id=1, source_target_pairs={{0,1},{1,2},{2,3},{3,4},{4,5},{5,6},{6,7},{7,8},{8,9},{9,10},{10,1... | collective-permute-start | bytes 786440 | tf_op jit(solution)/shard_map/ppermute | solution.py:12
  47.9 9.4 %collective-permute-start.3 = (bf16[4,2,1,32,256]{4,3,2,1,0:T(8,128)(2,1)}, bf16[4,2,1,32,256]{4,3,2,1,0:T(8,128)(2,1)}, u32[]{:S(2)}, u32[]{:S(2)}) collective-permute-start(bf16[4,2,1,32,256]{4,3,2,1,0:T(8,128)(2,1)} %get-tuple-element.840), channel_id=1, source_target_pairs={{1,0},{2,1},{3,2},{4,3},{5,4},{6,5},{7,6},{8,7},{9,8},{10,9},{11,1... | collective-permute-start | bytes 393224 | tf_op jit(solution)/shard_map/ppermute | solution.py:15
  49.8 10.5 %collective-permute-start.2 = (bf16[4,2,1,32,256]{4,3,2,1,0:T(8,128)(2,1)}, bf16[4,2,1,32,256]{4,3,2,1,0:T(8,128)(2,1)}, u32[]{:S(2)}, u32[]{:S(2)}) collective-permute-start(bf16[4,2,1,32,256]{4,3,2,1,0:T(8,128)(2,1)} %get-tuple-element.839), channel_id=1, source_target_pairs={{0,1},{1,2},{2,3},{3,4},{4,5},{5,6},{6,7},{7,8},{8,9},{9,10},{10,1... | collective-permute-start | bytes 393224 | tf_op jit(solution)/shard_map/ppermute | solution.py:12
  67.8 10.5 %collective-permute-start.4 = (bf16[4,2,1,32,256]{4,3,2,1,0:T(8,128)(2,1)}, bf16[4,2,1,32,256]{4,3,2,1,0:T(8,128)(2,1)}, u32[]{:S(2)}, u32[]{:S(2)}) collective-permute-start(bf16[4,2,1,32,256]{4,3,2,1,0:T(8,128)(2,1)} %get-tuple-element.837), channel_id=1, source_target_pairs={{0,1},{1,2},{2,3},{3,4},{4,5},{5,6},{6,7},{7,8},{8,9},{9,10},{10,1... | collective-permute-start | bytes 393224 | tf_op jit(solution)/shard_map/ppermute | solution.py:12
  80.4 89.4 %collective-permute-start.6 = (bf16[4,2,4,32,256]{4,3,2,1,0:T(8,128)(2,1)}, bf16[4,2,4,32,256]{4,3,2,1,0:T(8,128)(2,1)}, u32[]{:S(2)}, u32[]{:S(2)}) collective-permute-start(bf16[4,2,4,32,256]{4,3,2,1,0:T(8,128)(2,1)} %get-tuple-element.1395), channel_id=1, source_target_pairs={{0,32},{32,64},{64,96},{1,33},{33,65},{65,97},{2,34},{34,66},{66,9... | collective-permute-start | bytes 1572872 | tf_op jit(solution)/shard_map/ppermute | solution.py:23
  174.1 11.9 %collective-permute-start.7 = (bf16[4,2,1,64,256]{4,3,2,1,0:T(8,128)(2,1)}, bf16[4,2,1,64,256]{4,3,2,1,0:T(8,128)(2,1)}, u32[]{:S(2)}, u32[]{:S(2)}) collective-permute-start(bf16[4,2,1,64,256]{4,3,2,1,0:T(8,128)(2,1)} %get-tuple-element.821), channel_id=1, source_target_pairs={{0,1},{1,2},{2,3},{3,4},{4,5},{5,6},{6,7},{7,8},{8,9},{9,10},{10,1... | collective-permute-start | bytes 786440 | tf_op jit(solution)/shard_map/ppermute | solution.py:12
  195.9 10.5 %collective-permute-start.9 = (bf16[4,2,1,32,256]{4,3,2,1,0:T(8,128)(2,1)}, bf16[4,2,1,32,256]{4,3,2,1,0:T(8,128)(2,1)}, u32[]{:S(2)}, u32[]{:S(2)}) collective-permute-start(bf16[4,2,1,32,256]{4,3,2,1,0:T(8,128)(2,1)} %get-tuple-element.835), channel_id=1, source_target_pairs={{0,1},{1,2},{2,3},{3,4},{4,5},{5,6},{6,7},{7,8},{8,9},{9,10},{10,1... | collective-permute-start | bytes 393224 | tf_op jit(solution)/shard_map/ppermute | solution.py:12
  237.1 10.5 %collective-permute-start.11 = (bf16[4,2,1,32,256]{4,3,2,1,0:T(8,128)(2,1)}, bf16[4,2,1,32,256]{4,3,2,1,0:T(8,128)(2,1)}, u32[]{:S(2)}, u32[]{:S(2)}) collective-permute-start(bf16[4,2,1,32,256]{4,3,2,1,0:T(8,128)(2,1)} %get-tuple-element.833), channel_id=1, source_target_pairs={{0,1},{1,2},{2,3},{3,4},{4,5},{5,6},{6,7},{7,8},{8,9},{9,10},{10,1... | collective-permute-start | bytes 393224 | tf_op jit(solution)/shard_map/ppermute | solution.py:12
  278.8 43.1 %collective-permute-start.13 = (bf16[4,2,4,32,256]{4,3,2,1,0:T(8,128)(2,1)}, bf16[4,2,4,32,256]{4,3,2,1,0:T(8,128)(2,1)}, u32[]{:S(2)}, u32[]{:S(2)}) collective-permute-start(bf16[4,2,4,32,256]{4,3,2,1,0:T(8,128)(2,1)} %get-tuple-element.1399), channel_id=1, source_target_pairs={{0,32},{32,64},{64,96},{1,33},{33,65},{65,97},{2,34},{34,66},{66,9... | collective-permute-start | bytes 1572872 | tf_op jit(solution)/shard_map/ppermute | solution.py:23
  325.6 11.9 %collective-permute-start.14 = (bf16[4,2,1,64,256]{4,3,2,1,0:T(8,128)(2,1)}, bf16[4,2,1,64,256]{4,3,2,1,0:T(8,128)(2,1)}, u32[]{:S(2)}, u32[]{:S(2)}) collective-permute-start(bf16[4,2,1,64,256]{4,3,2,1,0:T(8,128)(2,1)} %get-tuple-element.819), channel_id=1, source_target_pairs={{0,1},{1,2},{2,3},{3,4},{4,5},{5,6},{6,7},{7,8},{8,9},{9,10},{10,1... | collective-permute-start | bytes 786440 | tf_op jit(solution)/shard_map/ppermute | solution.py:12
  346.2 10.5 %collective-permute-start.16 = (bf16[4,2,1,32,256]{4,3,2,1,0:T(8,128)(2,1)}, bf16[4,2,1,32,256]{4,3,2,1,0:T(8,128)(2,1)}, u32[]{:S(2)}, u32[]{:S(2)}) collective-permute-start(bf16[4,2,1,32,256]{4,3,2,1,0:T(8,128)(2,1)} %get-tuple-element.831), channel_id=1, source_target_pairs={{0,1},{1,2},{2,3},{3,4},{4,5},{5,6},{6,7},{7,8},{8,9},{9,10},{10,1... | collective-permute-start | bytes 393224 | tf_op jit(solution)/shard_map/ppermute | solution.py:12
  349.6 89.1 %collective-permute-start.21 = (bf16[4,2,8,64,128]{4,3,2,1,0:T(8,128)(2,1)}, bf16[4,2,8,64,128]{4,3,2,1,0:T(8,128)(2,1)}, u32[]{:S(2)}, u32[]{:S(2)}) collective-permute-start(bf16[4,2,8,64,128]{4,3,2,1,0:T(8,128)(2,1)} %get-tuple-element.1392), channel_id=1, source_target_pairs={{0,96},{1,97},{2,98},{3,99},{4,100},{5,101},{6,102},{7,103},{8,104... | collective-permute-start | bytes 3145736 | tf_op jit(solution)/shard_map/ppermute | solution.py:23
  387.8 10.5 %collective-permute-start.18 = (bf16[4,2,1,32,256]{4,3,2,1,0:T(8,128)(2,1)}, bf16[4,2,1,32,256]{4,3,2,1,0:T(8,128)(2,1)}, u32[]{:S(2)}, u32[]{:S(2)}) collective-permute-start(bf16[4,2,1,32,256]{4,3,2,1,0:T(8,128)(2,1)} %get-tuple-element.829), channel_id=1, source_target_pairs={{0,1},{1,2},{2,3},{3,4},{4,5},{5,6},{6,7},{7,8},{8,9},{9,10},{10,1... | collective-permute-start | bytes 393224 | tf_op jit(solution)/shard_map/ppermute | solution.py:12
  429.5 9.2 %collective-permute-start.20 = (bf16[4,2,4,32,256]{4,3,2,1,0:T(8,128)(2,1)}, bf16[4,2,4,32,256]{4,3,2,1,0:T(8,128)(2,1)}, u32[]{:S(2)}, u32[]{:S(2)}) collective-permute-start(bf16[4,2,4,32,256]{4,3,2,1,0:T(8,128)(2,1)} %get-tuple-element.1404), channel_id=1, source_target_pairs={{0,32},{32,64},{64,96},{1,33},{33,65},{65,97},{2,34},{34,66},{66,9... | collective-permute-start | bytes 1572872 | tf_op jit(solution)/shard_map/ppermute | solution.py:23
  440.8 8.7 %collective-permute-start.23 = (bf16[4,2,1,64,256]{4,3,2,1,0:T(8,128)(2,1)}, bf16[4,2,1,64,256]{4,3,2,1,0:T(8,128)(2,1)}, u32[]{:S(2)}, u32[]{:S(2)}) collective-permute-start(bf16[4,2,1,64,256]{4,3,2,1,0:T(8,128)(2,1)} %get-tuple-element.818), channel_id=1, source_target_pairs={{1,0},{2,1},{3,2},{4,3},{5,4},{6,5},{7,6},{8,7},{9,8},{10,9},{11,1... | collective-permute-start | bytes 786440 | tf_op jit(solution)/shard_map/ppermute | solution.py:15
  442.7 13.2 %collective-permute-start.22 = (bf16[4,2,1,64,256]{4,3,2,1,0:T(8,128)(2,1)}, bf16[4,2,1,64,256]{4,3,2,1,0:T(8,128)(2,1)}, u32[]{:S(2)}, u32[]{:S(2)}) collective-permute-start(bf16[4,2,1,64,256]{4,3,2,1,0:T(8,128)(2,1)} %get-tuple-element.817), channel_id=1, source_target_pairs={{0,1},{1,2},{2,3},{3,4},{4,5},{5,6},{6,7},{7,8},{8,9},{9,10},{10,1... | collective-permute-start | bytes 786440 | tf_op jit(solution)/shard_map/ppermute | solution.py:12
  464.6 10.5 %collective-permute-start.24 = (bf16[4,2,1,32,256]{4,3,2,1,0:T(8,128)(2,1)}, bf16[4,2,1,32,256]{4,3,2,1,0:T(8,128)(2,1)}, u32[]{:S(2)}, u32[]{:S(2)}) collective-permute-start(bf16[4,2,1,32,256]{4,3,2,1,0:T(8,128)(2,1)} %get-tuple-element.827), channel_id=1, source_target_pairs={{0,1},{1,2},{2,3},{3,4},{4,5},{5,6},{6,7},{7,8},{8,9},{9,10},{10,1... | collective-permute-start | bytes 393224 | tf_op jit(solution)/shard_map/ppermute | solution.py:12
  480.9 10.5 %collective-permute-start.26 = (bf16[4,2,1,32,256]{4,3,2,1,0:T(8,128)(2,1)}, bf16[4,2,1,32,256]{4,3,2,1,0:T(8,128)(2,1)}, u32[]{:S(2)}, u32[]{:S(2)}) collective-permute-start(bf16[4,2,1,32,256]{4,3,2,1,0:T(8,128)(2,1)} %get-tuple-element.825), channel_id=1, source_target_pairs={{0,1},{1,2},{2,3},{3,4},{4,5},{5,6},{6,7},{7,8},{8,9},{9,10},{10,1... | collective-permute-start | bytes 393224 | tf_op jit(solution)/shard_map/ppermute | solution.py:12
  484.2 51.3 %collective-permute-start.29 = (bf16[4,2,8,64,128]{4,3,2,1,0:T(8,128)(2,1)}, bf16[4,2,8,64,128]{4,3,2,1,0:T(8,128)(2,1)}, u32[]{:S(2)}, u32[]{:S(2)}) collective-permute-start(bf16[4,2,8,64,128]{4,3,2,1,0:T(8,128)(2,1)} %bitcast.137), channel_id=1, source_target_pairs={{0,96},{1,97},{2,98},{3,99},{4,100},{5,101},{6,102},{7,103},{8,104... | collective-permute-start | bytes 3145736 | tf_op jit(solution)/shard_map/ppermute | solution.py:23
  493.5 42.0 %collective-permute-start.28 = (bf16[4,2,4,32,256]{4,3,2,1,0:T(8,128)(2,1)}, bf16[4,2,4,32,256]{4,3,2,1,0:T(8,128)(2,1)}, u32[]{:S(2)}, u32[]{:S(2)}) collective-permute-start(bf16[4,2,4,32,256]{4,3,2,1,0:T(8,128)(2,1)} %get-tuple-element.1409), channel_id=1, source_target_pairs={{0,32},{32,64},{64,96},{1,33},{33,65},{65,97},{2,34},{34,66},{66,9... | collective-permute-start | bytes 1572872 | tf_op jit(solution)/shard_map/ppermute | solution.py:23
  537.4 8.4 %collective-permute-start.31 = (bf16[4,2,1,64,256]{4,3,2,1,0:T(8,128)(2,1)}, bf16[4,2,1,64,256]{4,3,2,1,0:T(8,128)(2,1)}, u32[]{:S(2)}, u32[]{:S(2)}) collective-permute-start(bf16[4,2,1,64,256]{4,3,2,1,0:T(8,128)(2,1)} %get-tuple-element.816), channel_id=1, source_target_pairs={{1,0},{2,1},{3,2},{4,3},{5,4},{6,5},{7,6},{8,7},{9,8},{10,9},{11,1... | collective-permute-start | bytes 786440 | tf_op jit(solution)/shard_map/ppermute | solution.py:15
  539.5 11.9 %collective-permute-start.30 = (bf16[4,2,1,64,256]{4,3,2,1,0:T(8,128)(2,1)}, bf16[4,2,1,64,256]{4,3,2,1,0:T(8,128)(2,1)}, u32[]{:S(2)}, u32[]{:S(2)}) collective-permute-start(bf16[4,2,1,64,256]{4,3,2,1,0:T(8,128)(2,1)} %get-tuple-element.815), channel_id=1, source_target_pairs={{0,1},{1,2},{2,3},{3,4},{4,5},{5,6},{6,7},{7,8},{8,9},{9,10},{10,1... | collective-permute-start | bytes 786440 | tf_op jit(solution)/shard_map/ppermute | solution.py:12
  (32 other events, 148.5 us)
Sparse Core Ops, SparseCore 0:
  561.5 67.3 reduce-scatter.3
where the time goes:
time: 648 us; the launch traced here: 638 us
  waiting for transfers between devices  272 us (42%)
  starting transfers between devices  117 us (18%)
  local copies, waits for them, and re-layouts  115 us (18%)
  matrix products  60.3 us (9%)
  other arithmetic  53.6 us (8%)
  between operations  15 us (2%)
    ppermute x6, waiting for transfers between devices, from_behind(): return lax.ppermute(value, axis, pairs)  110 us
    ppermute x13, waiting for transfers between devices, extended(): lax.ppermute(lax.slice_in_dim(block, block.shape[dim] - width, None, axis...  79.6 us
    unnamed x2, waiting for transfers between devices  67.4 us
    ppermute x6, starting transfers between devices, from_behind(): return lax.ppermute(value, axis, pairs)  43.9 us
    ppermute x13, starting transfers between devices, extended(): lax.ppermute(lax.slice_in_dim(block, block.shape[dim] - width, None, axis...  40.6 us
    concatenate x13, other arithmetic, extended(): block = jnp.concatenate([low, block, high], axis=dim)  34.9 us
    ppermute x13, starting transfers between devices, extended(): lax.ppermute(lax.slice_in_dim(block, 0, width, axis=dim), axis, backward)  32.6 us
    dot_general x5, matrix products, embed_fields(): jnp.einsum('bzyxf,fc->bzyxc', feats, embed_w, precision=lax.Precision.HIG...  31.5 us
  transfers between devices with their start and end apart: 33, of which 25 were waited for; matrix products, arithmetic and copies ran while one was open for 15% of the time, Pallas kernels for 0%

commit v1 on v0

v1 whole, which is shorter than its diff:
```python
import jax
import jax.numpy as jnp
from jax import lax
from jax.experimental import pallas as pl
from jax.experimental.pallas import tpu as pltpu
from jax.sharding import PartitionSpec as P

F32 = jnp.float32
BF16 = jnp.bfloat16
AXES = ("segment", "space")
SEGMENTS = 4
TILES = 32
GROUP = 4
VMEM_LIMIT = 60 * 1024 * 1024
R1 = 6
R2 = 8


def gelu(x):
    half = 0.5 * x
    t = jnp.tanh(x * (0.7978845608028654 + 0.035677408136300125 * (x * x)))
    return half + half * t


def nn(a, b):
    return lax.dot_general(a, b, (((1,), (0,)), ((), ())), preferred_element_type=F32)


def nt(a, b):
    return lax.dot_general(a, b, (((1,), (1,)), ((), ())), preferred_element_type=F32)


def iota(shape, dim):
    return lax.broadcasted_iota(jnp.int32, shape, dim)


def member_of(segment, space):
    return segment ^ (2 * ((space // GROUP) % 2))


def pack_kernel(state_ref, noise_ref, land_ref, out_ref, even_ref, odd_ref):
    member = member_of(lax.axis_index("segment"), lax.axis_index("space"))
    even_ref[...] = jnp.zeros_like(even_ref)
    odd_ref[...] = jnp.zeros_like(odd_ref)
    for m in range(2):
        for lev in range(2):
            for y in range(8):
                dst = even_ref if y % 2 == 0 else odd_ref
                row = ((m * 4 + y // 2) * 2 + lev) * 8
                dst[pl.ds(row, 5), :] = state_ref[pl.ds(m * 80 + lev * 8 + y, 5, stride=16), :]
                dst[pl.ds(row + 5, 1), :] = noise_ref[m, member, lev, pl.ds(y, 1), :]
                dst[pl.ds(row + 6, 1), :] = land_ref[pl.ds(y, 1), :].astype(F32)
    total = jnp.zeros((128, 128), F32)
    for ylo, ref in ((0, even_ref), (1, odd_ref)):
        x = iota((64, 128), 0)
        lane = iota((64, 128), 1)
        spread = jnp.where(lane == (x % 2) * 64 + ylo * 32 + x // 2, 1.0, 0.0).astype(BF16)
        rest = ref[...]
        for _ in range(3):
            part = rest.astype(BF16)
            total = total + nn(part, spread)
            rest = rest - part.astype(F32)
    for z in range(GROUP):
        out_ref[z] = total[(z % 2) * 64 : (z % 2) * 64 + 64]


def shift_down(v):
    keep = iota(v.shape, 0) % 32 != 0
    return jnp.where(keep, pltpu.roll(v, 1, 0), 0.0)


def shift_up(v):
    keep = iota(v.shape, 0) % 32 != 31
    return jnp.where(keep, pltpu.roll(v, v.shape[0] - 1, 0), 0.0)


def net_kernel(
    local_ref,
    rim_ref,
    embed_ref,
    merge_ref,
    expand_ref,
    head_ref,
    fine_hbm,
    coarse_hbm,
    out_ref,
    fine_w,
    coarse_w,
    ew_ref,
    f_ref,
    ee,
    eo,
    es1,
    es2,
    de,
    do,
    ds1,
    ds2,
    ca,
    cb,
    sems,
):
    space = lax.axis_index("space")
    upper = (space // 2) % 2 == 1
    first = space < 2
    last = space >= TILES - 2

    copies = [pltpu.make_async_copy(fine_hbm.at[0], fine_w.at[0], sems.at[0])]
    for k in range(4):
        copies.append(pltpu.make_async_copy(coarse_hbm.at[k], coarse_w.at[k], sems.at[1 + k]))
    copies.append(pltpu.make_async_copy(fine_hbm.at[1], fine_w.at[1], sems.at[5]))
    for copy in copies:
        copy.start()

    for j in range(20):
        low = rim_ref[pl.ds(j * 16, 16), :] if j < 6 else local_ref[pl.ds((j - 6) * 16, 16), :]
        high = (
            local_ref[pl.ds((j + 2) * 16, 16), :] if j < 14 else rim_ref[pl.ds((j - 14) * 16, 16), :]
        )
        f_ref[pl.ds(j * 16, 16), :] = jnp.where(upper, high, low)

    ew_ref[...] = jnp.zeros_like(ew_ref)
    ew_ref[pl.ds(0, 7), :] = embed_ref[...]
    w = ew_ref[...]
    w_hi = w.astype(BF16).astype(F32)
    w_lo = w - w_hi
    w4 = jnp.concatenate([w_hi, w_hi, w_lo, w_lo], axis=0).astype(BF16)

    per = 4
    def embed_block(i, _):
        for lev in range(2):
            parts = []
            for j in range(per):
                t = f_ref[pl.ds(pl.multiple_of((i * per + j) * 16 + lev * 8, 8), 8), :]
                hi = t.astype(BF16).astype(F32)
                lo = t - hi
                parts.append(jnp.concatenate([hi, lo, hi, lo], axis=0).T)
            feats = jnp.concatenate(parts, axis=0).astype(BF16)
            g = gelu(nn(feats, w4))
            even = jnp.concatenate([g[j * 128 : j * 128 + 64] for j in range(per)], axis=0)
            odd = jnp.concatenate([g[j * 128 + 64 : j * 128 + 128] for j in range(per)], axis=0)
            rows = pl.ds(pl.multiple_of(i * per * 64, 64), per * 64)
            lanes = pl.ds(lev * 256, 256)
            ee[rows, lanes] = even.astype(BF16)
            eo[rows, lanes] = odd.astype(BF16)
            es1[rows, lanes] = shift_down(odd).astype(BF16)
            es2[rows, lanes] = shift_up(even).astype(BF16)
        return 0

    lax.fori_loop(0, 20 // per, embed_block, 0)

    def fine_conv(layer, row, n, srcs):
        e, o, s1, s2 = srcs
        sides = ((s1, e), (e, o), (o, s2))
        acc = None
        for dy in range(3):
            for dx in range(3):
                rows = pl.ds((row + dy) * 32, n * 32)
                a, b = sides[dx]
                lhs = jnp.concatenate([a[rows, :], b[rows, :]], axis=0)
                taps = [
                    fine_w[layer, pl.ds(((dz * 3 + dy) * 3 + dx) * 256, 256), :] for dz in range(3)
                ]
                rhs = jnp.concatenate(
                    [
                        jnp.concatenate([taps[1], taps[0]], axis=1),
                        jnp.concatenate([taps[2], taps[1]], axis=1),
                    ],
                    axis=0,
                )
                term = nn(lhs, rhs)
                acc = term if acc is None else acc + term
        return acc

    copies[0].wait()
    for blk in range(36 // R1):
        row = blk * R1
        g = gelu(fine_conv(0, row + 1, R1, (ee, eo, es1, es2)))
        even, odd = g[: R1 * 32], g[R1 * 32 :]
        rows = pl.ds(row * 32, R1 * 32)
        odd_s, even_s = shift_down(odd), shift_up(even)
        for lev in range(2):
            src = slice(lev * 128, lev * 128 + 128)
            dst = pl.ds(lev * 256 + 128, 128)
            de[rows, dst] = even[:, src].astype(BF16)
            do[rows, dst] = odd[:, src].astype(BF16)
            ds1[rows, dst] = odd_s[:, src].astype(BF16)
            ds2[rows, dst] = even_s[:, src].astype(BF16)

    @pl.when(first)
    def _():
        for ref in (de, do, ds1, ds2):
            ref[pl.ds(0, 320), :] = jnp.zeros((320, 512), BF16)

    @pl.when(last)
    def _():
        for ref in (de, do, ds1, ds2):
            ref[pl.ds(26 * 32, 320), :] = jnp.zeros((320, 512), BF16)

    def keep_coarse(dst, lev, v):
        lanes = pl.ds(lev * 256, 256)
        rows = pl.ds(0, v.shape[0])
        dst[1, rows, lanes] = v.astype(BF16)
        dst[0, rows, lanes] = shift_down(v).astype(BF16)
        dst[2, rows, lanes] = shift_up(v).astype(BF16)

    for lev in range(2):
        lanes = pl.ds(lev * 256 + 128, 128)
        pieces = [
            jnp.concatenate([ref[pl.ds((2 * r + dy) * 32, 32), lanes] for r in range(18)], axis=0)
            for dy in range(2)
            for ref in (de, do)
        ]
        keep_coarse(ca, lev, gelu(nn(jnp.concatenate(pieces, axis=1), merge_ref[...])))

    src, dst = ca, cb
    for k in range(4):
        n = 16 - 2 * k
        copies[1 + k].wait()
        acc = [None, None]
        for dy in range(3):
            for dx in range(3):
                lhs = src[dx, pl.ds(dy * 32, n * 32), :]
                taps = [
                    coarse_w[k, pl.ds(((dz * 3 + dy) * 3 + dx) * 256, 256), :] for dz in range(3)
                ]
                for lev in range(2):
                    rhs = jnp.concatenate(
                        [taps[1], taps[2]] if lev == 0 else [taps[0], taps[1]], axis=0
                    )
                    term = nn(lhs, rhs)
                    acc[lev] = term if acc[lev] is None else acc[lev] + term
        for lev in range(2):
            before = src[1, pl.ds(32, n * 32), pl.ds(lev * 256, 256)].astype(F32)
            keep_coarse(dst, lev, before + gelu(acc[lev]))
        edge = 4 - k

        @pl.when(first)
        def _(dst=dst, edge=edge):
            dst[:, pl.ds(0, edge * 32), :] = jnp.zeros((3, edge * 32, 512), BF16)

        @pl.when(last)
        def _(dst=dst, edge=edge, n=n):
            dst[:, pl.ds((n - edge) * 32, edge * 32), :] = jnp.zeros((3, edge * 32, 512), BF16)

        src, dst = dst, src

    for lev in range(2):
        up = nn(src[1, pl.ds(0, 320), pl.ds(lev * 256, 256)], expand_ref[...])
        lanes = pl.ds(lev * 256, 128)
        down, high = shift_down(up), shift_up(up)
        for d in range(18):
            r, dy = (d + 1) // 2, (d + 1) % 2
            rows = pl.ds((d + 9) * 32, 32)
            even = slice(dy * 256, dy * 256 + 128)
            odd = slice(dy * 256 + 128, dy * 256 + 256)
            here = slice(r * 32, r * 32 + 32)
            de[rows, lanes] = up[here, even].astype(BF16)
            do[rows, lanes] = up[here, odd].astype(BF16)
            ds1[rows, lanes] = down[here, odd].astype(BF16)
            ds2[rows, lanes] = high[here, even].astype(BF16)

    row_id = iota((16, 5), 0)
    var_id = iota((16, 5), 1)
    head = jnp.concatenate(
        [
            nt(jnp.where(row_id == 2 * var_id + lev, 1.0, 0.0).astype(BF16), head_ref[...])
            for lev in range(2)
        ],
        axis=1,
    ).astype(BF16)

    src_lane = iota((512, 512), 0)
    dst_lane = iota((512, 512), 1)
    lon = 2 * (src_lane % 32) + src_lane // 256
    lat = (src_lane // 32) % 8
    spread = jnp.where(dst_lane == (lon // 16) * 128 + lat * 16 + lon % 16, 1.0, 0.0).astype(BF16)

    copies[5].wait()
    for half in range(2):
        evens, odds = [], []
        for blk in range(8 // R2):
            row = half * 8 + blk * R2
            g = gelu(fine_conv(1, row + 9, R2, (de, do, ds1, ds2))).astype(BF16)
            evens.append(g[: R2 * 32])
            odds.append(g[R2 * 32 :])
        add = nt(head, jnp.concatenate(evens + odds, axis=0))
        hi = add.astype(BF16)
        lo = (add - hi.astype(F32)).astype(BF16)
        both = nn(jnp.concatenate([hi, lo], axis=0), spread)
        both = both[:16] + both[16:]
        for s in range(SEGMENTS):
            out_ref[s * 2 + half] = both[:, s * 128 : s * 128 + 128]


def score_kernel(got_ref, state_ref, truth_ref, pred_ref, crps_ref):
    segment = lax.axis_index("segment")
    space = lax.axis_index("space")
    lane = iota((10, 128), 1)

    def block_rows(ref, start, lanes_from):
        total = jnp.zeros((10, 128), F32)
        for y in range(8):
            v = ref[pl.ds(start + y, 10, stride=8), :]
            v = jnp.concatenate([v, jnp.zeros((10, 128 - v.shape[1]), F32)], axis=1)
            v = pltpu.roll(v, lax.rem(y * 16 - lanes_from + 128, 128), 1)
            total = jnp.where(lane // 16 == y, v, total)
        return total

    def put(ref, start, v):
        for y in range(8):
            w = pltpu.roll(v, (128 - 16 * y) % 128, 1) if y else v
            ref[pl.ds(start + y, 10, stride=8), :] = w[:, :16]

    for m in range(2):
        state = block_rows(state_ref, m * 80, segment * 16)
        truth = block_rows(truth_ref, m * 80, 0)
        preds = []
        for b in range(4):
            src = member_of(b, space) * 2 + m
            preds.append(got_ref[src][:10] + state)
            put(pred_ref, (m * 4 + b) * 80, preds[b])
        skill = sum(jnp.abs(p - truth) for p in preds) * 0.25
        spread = sum(
            jnp.abs(preds[b] - preds[c]) for b in range(4) for c in range(b + 1, 4)
        )
        put(crps_ref, m * 80, skill - spread * (1.0 / 12.0))


def index(segment, column, z):
    return segment * TILES + column * GROUP + z


def body(
    state,
    noise,
    land_sea,
    observed_truth,
    embed_w,
    fine_weight_kernels,
    merge_w,
    coarse_w,
    expand_w,
    head_w,
):
    space = lax.axis_index("space")
    columns = TILES // GROUP
    state_rows = state.reshape(160, 64)
    params = pltpu.CompilerParams(vmem_limit_bytes=VMEM_LIMIT)
    vmem = pl.BlockSpec(memory_space=pltpu.VMEM)
    hbm = pl.BlockSpec(memory_space=pl.ANY)

    packed = pl.pallas_call(
        pack_kernel,
        out_shape=jax.ShapeDtypeStruct((GROUP, 64, 128), F32),
        in_specs=[vmem] * 3,
        out_specs=vmem,
        scratch_shapes=[pltpu.VMEM((128, 64), F32), pltpu.VMEM((128, 64), F32)],
        name="pack",
    )(state_rows, noise, land_sea)

    rings = [
        [index(s, c, z) for z in range(GROUP)] for s in range(SEGMENTS) for c in range(columns)
    ]
    local = lax.all_to_all(packed, AXES, 0, 0, axis_index_groups=rings, tiled=True)
    local = local.reshape(256, 128)

    pairs = []
    for s in range(SEGMENTS):
        for c in range(1, columns):
            for z in range(2):
                here, there = index(s, c, z), index(s ^ 2, c - 1, z + 2)
                pairs += [(here, there), (there, here)]
    upper = (space // 2) % 2
    rim = lax.ppermute(jnp.where(upper == 1, local[160:256], local[0:96]), AXES, pairs)

    e_buf = pltpu.VMEM((40 * 32, 512), BF16)
    d_buf = pltpu.VMEM((36 * 32, 512), BF16)
    increments = pl.pallas_call(
        net_kernel,
        out_shape=jax.ShapeDtypeStruct((8, 16, 128), F32),
        in_specs=[vmem] * 6 + [hbm] * 2,
        out_specs=vmem,
        scratch_shapes=[
            pltpu.VMEM((2, 6912, 128), BF16),
            pltpu.VMEM((4, 6912, 256), BF16),
            pltpu.VMEM((8, 256), F32),
            pltpu.VMEM((320, 128), F32),
            *[e_buf] * 4,
            *[d_buf] * 4,
            pltpu.VMEM((3, 576, 512), BF16),
            pltpu.VMEM((3, 576, 512), BF16),
            pltpu.SemaphoreType.DMA((6,)),
        ],
        compiler_params=params,
        name="net",
    )(local, rim, embed_w, merge_w, expand_w, head_w, fine_weight_kernels, coarse_w)

    squares = [
        [index(s, c, 2 * h + r) for s in range(SEGMENTS) for r in range(2)]
        for c in range(columns)
        for h in range(2)
    ]
    got = lax.all_to_all(increments, AXES, 0, 0, axis_index_groups=squares, tiled=True)

    prediction, crps = pl.pallas_call(
        score_kernel,
        out_shape=(
            jax.ShapeDtypeStruct((640, 16), F32),
            jax.ShapeDtypeStruct((160, 16), F32),
        ),
        in_specs=[vmem] * 3,
        out_specs=(vmem, vmem),
        name="score",
    )(got, state_rows, observed_truth.reshape(160, 16))
    return prediction.reshape(2, 4, 5, 2, 8, 16), crps.reshape(2, 5, 2, 8, 16)


def solution(mesh):
    return jax.shard_map(
        body,
        mesh=mesh,
        in_specs=(
            P(None, None, None, "space", None),
            P(None, None, None, "space", None),
            P("space", None),
            P(None, None, None, "space", "segment"),
            P(),
            P(),
            P(),
            P(),
            P(),
            P(),
        ),
        out_specs=(
            P(None, None, None, None, "space", "segment"),
            P(None, None, None, "space", "segment"),
        ),
        check_vma=False,
    )
```

time: 648 us -> 65.3 us (0.10); the launches traced: 638 us -> 64.9 us
  waiting for transfers between devices: 272 us -> 8.24 us
  local copies, waits for them, and re-layouts: 115 us -> 2.02 us
  starting transfers between devices: 117 us -> 9.55 us
  matrix products: 60.3 us -> 0 us
  other arithmetic: 53.6 us -> 0.01 us
  Pallas kernels: 0 us -> 32.9 us
  between operations: 15 us -> 0.66 us
  blocking collectives: 0 us -> 11.6 us
    ppermute x32 -> x1, waiting for transfers between devices: 204 us -> 3.41 us  [body(): lax.ppermute(jnp.where(upper == 1, local[160:256], local[0:96]), AXES, pa...]
    ppermute x32 -> x1, starting transfers between devices: 117 us -> 4.53 us  [body(): lax.ppermute(jnp.where(upper == 1, local[160:256], local[0:96]), AXES, pa...]
    unnamed x2 -> x0, waiting for transfers between devices: 67.4 us -> none
    dot_general x21 -> x0, matrix products: 60.3 us -> none  [the longest x5 31.5 us: embed_fields(): jnp.einsum('bzyxf,fc->bzyxc', feats, embed_w, precision=lax.Precision.HIG...]
    concatenate x13 -> x0, other arithmetic: 34.9 us -> none  [extended(): block = jnp.concatenate([low, block, high], axis=dim)]
    pallas_call x0 -> x3, Pallas kernels: none -> 32.9 us  [the longest x1 28.9 us: body(): pl.pallas_call(net_kernel, out_shape=jax.ShapeDtypeStruct((8, 16, 128), F...]
    squeeze x20 -> x0, local copies, waits for them, and re-layouts: 29.2 us -> none  [the longest x16 17 us: conv_layer(): return lax.map(lambda member: conv_member(member, weight), padded)]
    while x448 -> x0, local copies, waits for them, and re-layouts: 28.1 us -> none
  transfers between devices with their start and end apart: 33 -> 2, of which waited for: 25 -> 2; matrix products, arithmetic and copies ran while one was open for 15% -> 2% of each run, Pallas kernels for 0% -> 0%
where the time goes in v1:
time: 65.3 us; the launch traced here: 64.9 us
  Pallas kernels  32.9 us (50%)
  blocking collectives  11.6 us (18%)
  starting transfers between devices  9.55 us (15%)
  waiting for transfers between devices  8.24 us (13%)
  local copies, waits for them, and re-layouts  2.02 us (3%)
  between operations  0.66 us (1%)
    pallas_call x1, Pallas kernels, body(): pl.pallas_call(net_kernel, out_shape=jax.ShapeDtypeStruct((8, 16, 128), F...  28.9 us
    all_to_all x1, blocking collectives, body(): lax.all_to_all(increments, AXES, 0, 0, axis_index_groups=squares, tiled=T...  11.6 us
    all_to_all x1, starting transfers between devices, body(): lax.all_to_all(packed, AXES, 0, 0, axis_index_groups=rings, tiled=True)  5.02 us
    all_to_all x1, waiting for transfers between devices, body(): lax.all_to_all(packed, AXES, 0, 0, axis_index_groups=rings, tiled=True)  4.83 us
    ppermute x1, starting transfers between devices, body(): lax.ppermute(jnp.where(upper == 1, local[160:256], local[0:96]), AXES, pa...  4.53 us
    ppermute x1, waiting for transfers between devices, body(): lax.ppermute(jnp.where(upper == 1, local[160:256], local[0:96]), AXES, pa...  3.41 us
    pallas_call x1, Pallas kernels, body(): pl.pallas_call(score_kernel, out_shape=(jax.ShapeDtypeStruct((640, 16), F...  2.08 us
    unnamed x5, local copies, waits for them, and re-layouts  2.02 us
  transfers between devices with their start and end apart: 2, of which 2 were waited for; matrix products, arithmetic and copies ran while one was open for 2% of the time, Pallas kernels for 0%

profile of v1, /device:TPU:17, one launch (start us, length us, event | category | flops | bytes accessed | tf_op | source)
XLA Modules:
  0.0 64.9 jit_solution(15864620752857120011)
XLA Ops:
  0.6 1.8 %pack.1 = f32[4,64,128]{2,1,0:T(8,128)} custom-call(f32[160,64]{1,0:T(8,128)} %bitcast.7, f32[2,4,2,8,64]{4,3,2,1,0:T(8,128)} %noise_ref.1, s32[8,64]{1,0:T(8,128)} %land_ref.1), custom_call_target="tpu_custom_call" | custom-call | tf_op jit(solution)/shard_map/pack/pallas_call | solution.py:353
  2.5 5.0 %all-to-all-start = ((f32[4,64,128]{2,1,0:T(8,128)}), f32[4,64,128]{2,1,0:T(8,128)S(1)}, u32[]{:S(2)}, u32[]{:S(2)}) async-start(f32[4,64,128]{2,1,0:T(8,128)} %pack.1), calls=%async_computation | async-start | bytes 262144 | tf_op jit(solution)/shard_map/all_to_all | solution.py:365
  7.5 4.8 %all-to-all-done = f32[4,64,128]{2,1,0:T(8,128)S(1)} async-done(((f32[4,64,128]{2,1,0:T(8,128)}), f32[4,64,128]{2,1,0:T(8,128)S(1)}, u32[]{:S(2)}, u32[]{:S(2)}) %all-to-all-start) | async-done | bytes 131104 | tf_op jit(solution)/shard_map/all_to_all | solution.py:365
  12.3 0.0 copy-start
  12.3 4.5 %collective-permute-start = (f32[96,128]{1,0:T(8,128)S(1)}, f32[96,128]{1,0:T(8,128)S(1)}, u32[]{:S(2)}, u32[]{:S(2)}) collective-permute-start(f32[96,128]{1,0:T(8,128)S(1)} %slice_select_fusion), channel_id=1, source_target_pairs={{4,66},{66,4},{5,67},{67,5},{8,70},{70,8},{9,71},{71,9},{12,74},{7... | collective-permute-start | bytes 147464 | tf_op jit(solution)/shard_map/ppermute | solution.py:375
  16.9 1.4 %copy.12.head_ref = bf16[128,5]{1,0:T(8,128)(2,1)} copy(bf16[128,5]{0,1:T(8,128)(2,1)} %param.19) | data formatting | bytes 2560 | tf_op args[9]
  18.3 3.4 %collective-permute-done.rim_ref = f32[96,128]{1,0:T(8,128)S(1)} collective-permute-done((f32[96,128]{1,0:T(8,128)S(1)}, f32[96,128]{1,0:T(8,128)S(1)}, u32[]{:S(2)}, u32[]{:S(2)}) %collective-permute-start) | collective-permute-done | bytes 49184 | tf_op jit(solution)/shard_map/ppermute | solution.py:375
  21.7 0.0 copy-done
  21.7 0.0 copy-start.1
  21.7 0.6 copy-done.1
  22.3 28.9 %net.1 = f32[8,16,128]{2,1,0:T(8,128)} custom-call(f32[256,128]{1,0:T(8,128)} %bitcast.6, f32[96,128]{1,0:T(8,128)} %copy-done.1, f32[7,256]{1,0:T(8,128)} %embed_ref.1, bf16[512,256]{1,0:T(8,128)(2,1)} %merge_ref.1, bf16[256,512]{1,0:T(8,128)(2,1)} %expand_ref.1, bf16[128,5]{1,0:T(8,128)(2,1)} %copy.12.head_ref, bf16[2,6912,128]{2,1,0:T(8,128)(2,1)} %fine_hbm.1, ...), custom_call_target="tpu_custom_call" | custom-call | tf_op jit(solution)/shard_map/net/pallas_call | solution.py:379
  51.2 11.6 %all_to_all.10.got_ref = f32[8,16,128]{2,1,0:T(8,128)} all-to-all(f32[8,16,128]{2,1,0:T(8,128)} %net.1), channel_id=1, replica_groups={{0,1,32,33,64,65,96,97},{2,3,34,35,66,67,98,99},{4,5,36,37,68,69,100,10..., dimensions={0} | all-to-all | bytes 131072 | tf_op jit(solution)/shard_map/all_to_all | solution.py:404
  62.8 2.1 %score.1 = (f32[640,16]{1,0:T(8,128)}, f32[160,16]{1,0:T(8,128)}) custom-call(f32[8,16,128]{2,1,0:T(8,128)} %all_to_all.10.got_ref, f32[160,64]{1,0:T(8,128)} %bitcast.8, f32[160,16]{1,0:T(8,128)} %bitcast.9), custom_call_target="tpu_custom_call" | custom-call | tf_op jit(solution)/shard_map/score/pallas_call | solution.py:406
  (1 shorter events, 0.0 us)
Async XLA Ops:
  2.5 9.8 %all-to-all-start = ((f32[4,64,128]{2,1,0:T(8,128)}), f32[4,64,128]{2,1,0:T(8,128)S(1)}, u32[]{:S(2)}, u32[]{:S(2)}) async-start(f32[4,64,128]{2,1,0:T(8,128)} %pack.1), calls=%async_computation | async-start | bytes 262144 | tf_op jit(solution)/shard_map/all_to_all | solution.py:365
  12.3 9.4 %copy-start = (f32[4,64,128]{2,1,0:T(8,128)}, f32[4,64,128]{2,1,0:T(8,128)S(1)}, u32[]{:S(2)}) copy-start(f32[4,64,128]{2,1,0:T(8,128)S(1)} %all-to-all-done) | copy-start | bytes 393220
  12.3 9.3 %collective-permute-start = (f32[96,128]{1,0:T(8,128)S(1)}, f32[96,128]{1,0:T(8,128)S(1)}, u32[]{:S(2)}, u32[]{:S(2)}) collective-permute-start(f32[96,128]{1,0:T(8,128)S(1)} %slice_select_fusion), channel_id=1, source_target_pairs={{4,66},{66,4},{5,67},{67,5},{8,70},{70,8},{9,71},{71,9},{12,74},{7... | collective-permute-start | bytes 147464 | tf_op jit(solution)/shard_map/ppermute | solution.py:375
  21.7 0.6 copy-start.1

commit v2 on v1

--- a/solution.py
+++ b/solution.py
@@ -11,9 +11,11 @@
 SEGMENTS = 4
 TILES = 32
 GROUP = 4
-VMEM_LIMIT = 60 * 1024 * 1024
+VMEM_LIMIT = 50 * 1024 * 1024
+SMALL_LIMIT = 8 * 1024 * 1024
 R1 = 6
-R2 = 8
+RC = 1
+R2 = 4
 
 
 def gelu(x):
@@ -38,7 +40,7 @@
     return segment ^ (2 * ((space // GROUP) % 2))
 
 
-def pack_kernel(state_ref, noise_ref, land_ref, out_ref, even_ref, odd_ref):
+def pack_kernel(state_ref, noise_ref, land_ref, own_ref, other_ref, even_ref, odd_ref):
     member = member_of(lax.axis_index("segment"), lax.axis_index("space"))
     even_ref[...] = jnp.zeros_like(even_ref)
     odd_ref[...] = jnp.zeros_like(odd_ref)
@@ -60,8 +62,20 @@
             part = rest.astype(BF16)
             total = total + nn(part, spread)
             rest = rest - part.astype(F32)
-    for z in range(GROUP):
-        out_ref[z] = total[(z % 2) * 64 : (z % 2) * 64 + 64]
+    odd = lax.axis_index("space") % 2 == 1
+    own_ref[...] = jnp.where(odd, total[64:], total[:64])
+    other_ref[...] = jnp.where(odd, total[:64], total[64:])
+
+
+def join_kernel(own_ref, got_ref, pair_ref, near_ref, far_ref):
+    space = lax.axis_index("space")
+    odd = space % 2 == 1
+    upper = (space // 2) % 2 == 1
+    pair_ref[pl.ds(0, 64), :] = jnp.where(odd, got_ref[...], own_ref[...])
+    pair_ref[pl.ds(64, 64), :] = jnp.where(odd, own_ref[...], got_ref[...])
+    head, tail = pair_ref[pl.ds(0, 96), :], pair_ref[pl.ds(32, 96), :]
+    near_ref[...] = jnp.where(upper, head, tail)
+    far_ref[...] = jnp.where(upper, tail, head)
 
 
 def shift_down(v):
@@ -75,8 +89,9 @@
 
 
 def net_kernel(
-    local_ref,
-    rim_ref,
+    pair_ref,
+    near_ref,
+    far_ref,
     embed_ref,
     merge_ref,
     expand_ref,
@@ -112,12 +127,10 @@
     for copy in copies:
         copy.start()
 
-    for j in range(20):
-        low = rim_ref[pl.ds(j * 16, 16), :] if j < 6 else local_ref[pl.ds((j - 6) * 16, 16), :]
-        high = (
-            local_ref[pl.ds((j + 2) * 16, 16), :] if j < 14 else rim_ref[pl.ds((j - 14) * 16, 16), :]
-        )
-        f_ref[pl.ds(j * 16, 16), :] = jnp.where(upper, high, low)
+    near, far = near_ref[...], far_ref[...]
+    f_ref[pl.ds(0, 96), :] = jnp.where(upper, near, far)
+    f_ref[pl.ds(96, 128), :] = pair_ref[...]
+    f_ref[pl.ds(224, 96), :] = jnp.where(upper, far, near)
 
     ew_ref[...] = jnp.zeros_like(ew_ref)
     ew_ref[pl.ds(0, 7), :] = embed_ref[...]
@@ -197,9 +210,9 @@
         for ref in (de, do, ds1, ds2):
             ref[pl.ds(26 * 32, 320), :] = jnp.zeros((320, 512), BF16)
 
-    def keep_coarse(dst, lev, v):
+    def keep_coarse(dst, lev, v, start):
         lanes = pl.ds(lev * 256, 256)
-        rows = pl.ds(0, v.shape[0])
+        rows = pl.ds(start, v.shape[0])
         dst[1, rows, lanes] = v.astype(BF16)
         dst[0, rows, lanes] = shift_down(v).astype(BF16)
         dst[2, rows, lanes] = shift_up(v).astype(BF16)
@@ -211,28 +224,32 @@
             for dy in range(2)
             for ref in (de, do)
         ]
-        keep_coarse(ca, lev, gelu(nn(jnp.concatenate(pieces, axis=1), merge_ref[...])))
+        keep_coarse(ca, lev, gelu(nn(jnp.concatenate(pieces, axis=1), merge_ref[...])), 0)
 
     src, dst = ca, cb
     for k in range(4):
         n = 16 - 2 * k
         copies[1 + k].wait()
-        acc = [None, None]
-        for dy in range(3):
-            for dx in range(3):
-                lhs = src[dx, pl.ds(dy * 32, n * 32), :]
-                taps = [
-                    coarse_w[k, pl.ds(((dz * 3 + dy) * 3 + dx) * 256, 256), :] for dz in range(3)
-                ]
-                for lev in range(2):
-                    rhs = jnp.concatenate(
-                        [taps[1], taps[2]] if lev == 0 else [taps[0], taps[1]], axis=0
-                    )
-                    term = nn(lhs, rhs)
-                    acc[lev] = term if acc[lev] is None else acc[lev] + term
-        for lev in range(2):
-            before = src[1, pl.ds(32, n * 32), pl.ds(lev * 256, 256)].astype(F32)
-            keep_coarse(dst, lev, before + gelu(acc[lev]))
+        blocks = range(0, n, n // RC)
+        for row in blocks:
+            size = n // RC
+            acc = [None, None]
+            for dy in range(3):
+                for dx in range(3):
+                    lhs = src[dx, pl.ds((row + dy) * 32, size * 32), :]
+                    taps = [
+                        coarse_w[k, pl.ds(((dz * 3 + dy) * 3 + dx) * 256, 256), :]
+                        for dz in range(3)
+                    ]
+                    for lev in range(2):
+                        rhs = jnp.concatenate(
+                            [taps[1], taps[2]] if lev == 0 else [taps[0], taps[1]], axis=0
+                        )
+                        term = nn(lhs, rhs)
+                        acc[lev] = term if acc[lev] is None else acc[lev] + term
+            for lev in range(2):
+                before = src[1, pl.ds((row + 1) * 32, size * 32), pl.ds(lev * 256, 256)]
+                keep_coarse(dst, lev, before.astype(F32) + gelu(acc[lev]), row * 32)
         edge = 4 - k
 
         @pl.when(first)
@@ -264,7 +281,7 @@
     var_id = iota((16, 5), 1)
     head = jnp.concatenate(
         [
-            nt(jnp.where(row_id == 2 * var_id + lev, 1.0, 0.0).astype(BF16), head_ref[...])
+            nn(jnp.where(row_id == 2 * var_id + lev, 1.0, 0.0).astype(BF16), head_ref[...])
             for lev in range(2)
         ],
         axis=1,
@@ -327,59 +344,16 @@
         put(crps_ref, m * 80, skill - spread * (1.0 / 12.0))
 
 
-def index(segment, column, z):
-    return segment * TILES + column * GROUP + z
-
-
-def body(
-    state,
-    noise,
-    land_sea,
-    observed_truth,
-    embed_w,
-    fine_weight_kernels,
-    merge_w,
-    coarse_w,
-    expand_w,
-    head_w,
-):
-    space = lax.axis_index("space")
-    columns = TILES // GROUP
-    state_rows = state.reshape(160, 64)
+def run_net(pair, near, far, embed_w, merge_w, expand_w, head_w, fine_weight_kernels, coarse_w):
     params = pltpu.CompilerParams(vmem_limit_bytes=VMEM_LIMIT)
     vmem = pl.BlockSpec(memory_space=pltpu.VMEM)
     hbm = pl.BlockSpec(memory_space=pl.ANY)
-
-    packed = pl.pallas_call(
-        pack_kernel,
-        out_shape=jax.ShapeDtypeStruct((GROUP, 64, 128), F32),
-        in_specs=[vmem] * 3,
-        out_specs=vmem,
-        scratch_shapes=[pltpu.VMEM((128, 64), F32), pltpu.VMEM((128, 64), F32)],
-        name="pack",
-    )(state_rows, noise, land_sea)
-
-    rings = [
-        [index(s, c, z) for z in range(GROUP)] for s in range(SEGMENTS) for c in range(columns)
-    ]
-    local = lax.all_to_all(packed, AXES, 0, 0, axis_index_groups=rings, tiled=True)
-    local = local.reshape(256, 128)
-
-    pairs = []
-    for s in range(SEGMENTS):
-        for c in range(1, columns):
-            for z in range(2):
-                here, there = index(s, c, z), index(s ^ 2, c - 1, z + 2)
-                pairs += [(here, there), (there, here)]
-    upper = (space // 2) % 2
-    rim = lax.ppermute(jnp.where(upper == 1, local[160:256], local[0:96]), AXES, pairs)
-
     e_buf = pltpu.VMEM((40 * 32, 512), BF16)
     d_buf = pltpu.VMEM((36 * 32, 512), BF16)
     increments = pl.pallas_call(
         net_kernel,
         out_shape=jax.ShapeDtypeStruct((8, 16, 128), F32),
-        in_specs=[vmem] * 6 + [hbm] * 2,
+        in_specs=[vmem] * 7 + [hbm] * 2,
         out_specs=vmem,
         scratch_shapes=[
             pltpu.VMEM((2, 6912, 128), BF16),
@@ -394,7 +368,66 @@
         ],
         compiler_params=params,
         name="net",
-    )(local, rim, embed_w, merge_w, expand_w, head_w, fine_weight_kernels, coarse_w)
+    )(pair, near, far, embed_w, merge_w, expand_w, head_w, fine_weight_kernels, coarse_w)
+    return increments
+
+
+def index(segment, column, z):
+    return segment * TILES + column * GROUP + z
+
+
+def body(
+    state,
+    noise,
+    land_sea,
+    observed_truth,
+    embed_w,
+    fine_weight_kernels,
+    merge_w,
+    coarse_w,
+    expand_w,
+    head_w,
+):
+    columns = TILES // GROUP
+    state_rows = state.reshape(160, 64)
+    vmem = pl.BlockSpec(memory_space=pltpu.VMEM)
+
+    small = pltpu.CompilerParams(vmem_limit_bytes=SMALL_LIMIT)
+    tile = jax.ShapeDtypeStruct((64, 128), F32)
+    own, other = pl.pallas_call(
+        pack_kernel,
+        out_shape=(tile, tile),
+        in_specs=[vmem] * 3,
+        out_specs=(vmem, vmem),
+        scratch_shapes=[pltpu.VMEM((128, 64), F32), pltpu.VMEM((128, 64), F32)],
+        compiler_params=small,
+        name="pack",
+    )(state_rows, noise, land_sea)
+
+    every = [(s, c, z) for s in range(SEGMENTS) for c in range(columns) for z in range(GROUP)]
+    beside = [(index(s, c, z), index(s, c, z ^ 1)) for s, c, z in every]
+    across = [(index(s, c, z), index(s, c, z ^ 2)) for s, c, z in every]
+    beyond = []
+    for s, c, z in every:
+        if c > 0 and z < 2:
+            here, there = index(s, c, z), index(s ^ 2, c - 1, z + 2)
+            beyond += [(here, there), (there, here)]
+
+    got = lax.ppermute(other, AXES, beside)
+    rows12 = jax.ShapeDtypeStruct((96, 128), F32)
+    pair, near, far = pl.pallas_call(
+        join_kernel,
+        out_shape=(jax.ShapeDtypeStruct((128, 128), F32), rows12, rows12),
+        in_specs=[vmem] * 2,
+        out_specs=(vmem,) * 3,
+        compiler_params=small,
+        name="join",
+    )(own, got)
+    far = lax.ppermute(far, AXES, beyond)
+    near = lax.ppermute(near, AXES, across)
+    increments = run_net(
+        pair, near, far, embed_w, merge_w, expand_w, head_w.T, fine_weight_kernels, coarse_w
+    )
 
     squares = [
         [index(s, c, 2 * h + r) for s in range(SEGMENTS) for r in range(2)]
@@ -411,6 +444,7 @@
         ),
         in_specs=[vmem] * 3,
         out_specs=(vmem, vmem),
+        compiler_params=small,
         name="score",
     )(got, state_rows, observed_truth.reshape(160, 16))
     return prediction.reshape(2, 4, 5, 2, 8, 16), crps.reshape(2, 5, 2, 8, 16)

time: 65.3 us -> 58.8 us (0.900)
  Pallas kernels: 32.9 us -> 26.2 us
  local copies, waits for them, and re-layouts: 2.02 us -> 5.69 us
  waiting for transfers between devices: 8.24 us -> 6.62 us
  blocking collectives: 11.6 us -> 9.99 us
    pallas_call x2 -> x3, Pallas kernels: 30.8 us -> 25.1 us  [the longest x1 24.9 us: run_net(): pl.pallas_call(net_kernel, out_shape=jax.ShapeDtypeStruct((8, 16, 128), F...]
    all_to_all x1 -> x0, starting transfers between devices: 5.02 us -> none  [body(): lax.all_to_all(packed, AXES, 0, 0, axis_index_groups=rings, tiled=True)]
    all_to_all x1 -> x0, waiting for transfers between devices: 4.83 us -> none  [body(): lax.all_to_all(packed, AXES, 0, 0, axis_index_groups=rings, tiled=True)]
    ppermute x1 -> x3, starting transfers between devices: 4.53 us -> 9.22 us  [the longest x1 4 us: body(): far = lax.ppermute(far, AXES, beyond)]
    unnamed x5 -> x18, local copies, waits for them, and re-layouts: 2.02 us -> 5.69 us
    ppermute x1 -> x3, waiting for transfers between devices: 3.41 us -> 6.62 us  [the longest x1 5.31 us: body(): far = lax.ppermute(far, AXES, beyond)]
    all_to_all x1, blocking collectives: 11.6 us -> 9.99 us  [body(): lax.all_to_all(increments, AXES, 0, 0, axis_index_groups=squares, tiled=T...]
    pallas_call x1, Pallas kernels: 2.08 us -> 1.12 us  [body(): pl.pallas_call(score_kernel, out_shape=(jax.ShapeDtypeStruct((640, 16), F...]
  transfers between devices with their start and end apart: 2 -> 3, of which waited for: 2 -> 2; matrix products, arithmetic and copies ran while one was open for 2% -> 0% of each run, Pallas kernels for 0% -> 0%
where the time goes in v2:
time: 58.8 us; the launch traced here: 58.4 us
  Pallas kernels  26.2 us (45%)
  blocking collectives  9.99 us (17%)
  starting transfers between devices  9.22 us (16%)
  waiting for transfers between devices  6.62 us (11%)
  local copies, waits for them, and re-layouts  5.69 us (10%)
  between operations  0.69 us (1%)
    pallas_call x1, Pallas kernels, run_net(): pl.pallas_call(net_kernel, out_shape=jax.ShapeDtypeStruct((8, 16, 128), F...  24.9 us
    all_to_all x1, blocking collectives, body(): lax.all_to_all(increments, AXES, 0, 0, axis_index_groups=squares, tiled=T...  9.99 us
    unnamed x18, local copies, waits for them, and re-layouts  5.69 us
    ppermute x1, waiting for transfers between devices, body(): far = lax.ppermute(far, AXES, beyond)  5.31 us
    ppermute x1, starting transfers between devices, body(): far = lax.ppermute(far, AXES, beyond)  4 us
    ppermute x1, starting transfers between devices, body(): near = lax.ppermute(near, AXES, across)  3.5 us
    ppermute x1, starting transfers between devices, body(): got = lax.ppermute(other, AXES, beside)  1.72 us
    ppermute x1, waiting for transfers between devices, body(): got = lax.ppermute(other, AXES, beside)  1.3 us
  transfers between devices with their start and end apart: 3, of which 2 were waited for; matrix products, arithmetic and copies ran while one was open for 0% of the time, Pallas kernels for 0%

profile of v2, /device:TPU:17, one launch (start us, length us, event | category | flops | bytes accessed | tf_op | source)
XLA Modules:
  0.0 58.4 jit_solution(2946491036734165877)
XLA Ops:
  0.6 0.0 copy-start
  0.6 0.9 %copy-done = f32[2,5,2,8,64]{4,3,2,1,0:T(8,128)S(1)} copy-done((f32[2,5,2,8,64]{4,3,2,1,0:T(8,128)S(1)}, f32[2,5,2,8,64]{4,3,2,1,0:T(8,128)}, u32[]{:S(2)}) %copy-start) | copy-done | bytes 40984
  1.5 0.0 copy-start.5
  1.5 0.8 %copy-done.5 = f32[2,4,2,8,64]{4,3,2,1,0:T(8,128)S(1)} copy-done((f32[2,4,2,8,64]{4,3,2,1,0:T(8,128)S(1)}, f32[2,4,2,8,64]{4,3,2,1,0:T(8,128)}, u32[]{:S(2)}) %copy-start.5) | copy-done | bytes 32792
  2.4 0.0 copy-start.7
  2.4 0.7 %copy-done.7 = s32[8,64]{1,0:T(8,128)S(1)} copy-done((s32[8,64]{1,0:T(8,128)S(1)}, s32[8,64]{1,0:T(8,128)}, u32[]{:S(2)}) %copy-start.7) | copy-done | bytes 2072
  3.0 0.0 copy-start.1
  3.0 0.0 copy-start.4
  3.0 0.2 pack.1
  3.3 1.7 %collective-permute-start = (f32[64,128]{1,0:T(8,128)S(1)}, f32[64,128]{1,0:T(8,128)S(1)}, u32[]{:S(2)}, u32[]{:S(2)}) collective-permute-start(f32[64,128]{1,0:T(8,128)S(1)} %get-tuple-element.10), channel_id=1, source_target_pairs={{0,1},{1,0},{2,3},{3,2},{4,5},{5,4},{6,7},{7,6},{8,9},{9,8},{10,11... | collective-permute-start | bytes 98312 | tf_op jit(solution)/shard_map/ppermute | solution.py:416
  5.0 1.3 %collective-permute-done.got_ref = f32[64,128]{1,0:T(8,128)S(1)} collective-permute-done((f32[64,128]{1,0:T(8,128)S(1)}, f32[64,128]{1,0:T(8,128)S(1)}, u32[]{:S(2)}, u32[]{:S(2)}) %collective-permute-start) | collective-permute-done | bytes 32800 | tf_op jit(solution)/shard_map/ppermute | solution.py:416
  6.3 3.5 %collective-permute-start.1 = (f32[96,128]{1,0:T(8,128)S(1)}, f32[96,128]{1,0:T(8,128)S(1)}, u32[]{:S(2)}, u32[]{:S(2)}) collective-permute-start(f32[96,128]{1,0:T(8,128)S(1)} %get-tuple-element.12), channel_id=1, source_target_pairs={{0,2},{1,3},{2,0},{3,1},{4,6},{5,7},{6,4},{7,5},{8,10},{9,11},{10,... | collective-permute-start | bytes 147464 | tf_op jit(solution)/shard_map/ppermute | solution.py:427
  9.8 4.0 %collective-permute-start.2 = (f32[96,128]{1,0:T(8,128)S(1)}, f32[96,128]{1,0:T(8,128)S(1)}, u32[]{:S(2)}, u32[]{:S(2)}) collective-permute-start(f32[96,128]{1,0:T(8,128)S(1)} %get-tuple-element.13), channel_id=1, source_target_pairs={{4,66},{66,4},{5,67},{67,5},{8,70},{70,8},{9,71},{71,9},{12,74},{7... | collective-permute-start | bytes 147464 | tf_op jit(solution)/shard_map/ppermute | solution.py:426
  13.9 0.0 collective-permute-done.1.near_ref
  13.9 5.3 %collective-permute-done.2.far_ref = f32[96,128]{1,0:T(8,128)S(1)} collective-permute-done((f32[96,128]{1,0:T(8,128)S(1)}, f32[96,128]{1,0:T(8,128)S(1)}, u32[]{:S(2)}, u32[]{:S(2)}) %collective-permute-start.2) | collective-permute-done | bytes 49184 | tf_op jit(solution)/shard_map/ppermute | solution.py:426
  19.2 0.9 %copy-done.2 = bf16[512,256]{1,0:T(8,128)(2,1)S(1)} copy-done((bf16[512,256]{1,0:T(8,128)(2,1)S(1)}, bf16[512,256]{1,0:T(8,128)(2,1)}, u32[]{:S(2)}) %copy-start.2) | copy-done | bytes 262168
  20.1 0.9 %copy-done.3 = bf16[256,512]{1,0:T(8,128)(2,1)S(1)} copy-done((bf16[256,512]{1,0:T(8,128)(2,1)S(1)}, bf16[256,512]{1,0:T(8,128)(2,1)}, u32[]{:S(2)}) %copy-start.3) | copy-done | bytes 262168
  21.1 0.7 %copy-done.6 = f32[7,256]{1,0:T(8,128)S(1)} copy-done((f32[7,256]{1,0:T(8,128)S(1)}, f32[7,256]{1,0:T(8,128)}, u32[]{:S(2)}) %copy-start.6) | copy-done | bytes 7192
  21.8 0.7 %copy-done.8 = bf16[128,5]{0,1:T(8,128)(2,1)S(1)} copy-done((bf16[128,5]{0,1:T(8,128)(2,1)S(1)}, bf16[128,5]{0,1:T(8,128)(2,1)}, u32[]{:S(2)}) %copy-start.8) | copy-done | bytes 1304
  22.5 24.9 %net.1 = f32[8,16,128]{2,1,0:T(8,128)S(1)} custom-call(f32[128,128]{1,0:T(8,128)S(1)} %get-tuple-element.11.pair_ref, f32[96,128]{1,0:T(8,128)S(1)} %collective-permute-done.1.near_ref, f32[96,128]{1,0:T(8,128)S(1)} %collective-permute-done.2.far_ref, f32[7,256]{1,0:T(8,128)S(1)} %copy-done.6, bf16[512,256]{1,0:T(8,128)(2,1)S(1)} %copy-done.2, ...), custom_call_target="tpu_custom_call" | custom-call | tf_op jit(solution)/shard_map/net/pallas_call | solution.py:353
  47.3 10.0 %all_to_all.5.got_ref = f32[8,16,128]{2,1,0:T(8,128)S(1)} all-to-all(f32[8,16,128]{2,1,0:T(8,128)S(1)} %net.1), channel_id=1, replica_groups={{0,1,32,33,64,65,96,97},{2,3,34,35,66,67,98,99},{4,5,36,37,68,69,100,10..., dimensions={0} | all-to-all | bytes 131072 | tf_op jit(solution)/shard_map/all_to_all | solution.py:437
  57.3 0.0 copy-done.1
  57.3 0.0 copy-done.4
  57.3 1.1 %score.1 = (f32[640,16]{1,0:T(8,128)}, f32[160,16]{1,0:T(8,128)}) custom-call(f32[8,16,128]{2,1,0:T(8,128)S(1)} %all_to_all.5.got_ref, f32[160,64]{1,0:T(8,128)S(1)} %bitcast.6, f32[160,16]{1,0:T(8,128)S(1)} %bitcast.7), custom_call_target="tpu_custom_call" | custom-call | tf_op jit(solution)/shard_map/score/pallas_call | solution.py:439
  (5 shorter events, 0.0 us)
Async XLA Ops:
  0.6 0.9 %copy-start = (f32[2,5,2,8,64]{4,3,2,1,0:T(8,128)S(1)}, f32[2,5,2,8,64]{4,3,2,1,0:T(8,128)}, u32[]{:S(2)}) copy-start(f32[2,5,2,8,64]{4,3,2,1,0:T(8,128)} %param.10) | copy-start | bytes 122884
  1.5 0.8 %copy-start.5 = (f32[2,4,2,8,64]{4,3,2,1,0:T(8,128)S(1)}, f32[2,4,2,8,64]{4,3,2,1,0:T(8,128)}, u32[]{:S(2)}) copy-start(f32[2,4,2,8,64]{4,3,2,1,0:T(8,128)} %noise_ref.1) | copy-start | bytes 98308
  2.4 0.7 %copy-start.7 = (s32[8,64]{1,0:T(8,128)S(1)}, s32[8,64]{1,0:T(8,128)}, u32[]{:S(2)}) copy-start(s32[8,64]{1,0:T(8,128)} %land_ref.1) | copy-start | bytes 6148
  3.0 54.3 %copy-start.1 = (f32[2,5,2,8,64]{4,3,2,1,0:T(8,128)S(1)}, f32[2,5,2,8,64]{4,3,2,1,0:T(8,128)}, u32[]{:S(2)}) copy-start(f32[2,5,2,8,64]{4,3,2,1,0:T(8,128)} %param.10) | copy-start | bytes 122884
  3.0 54.3 %copy-start.4 = (f32[2,5,2,8,16]{4,3,2,1,0:T(8,128)S(1)}, f32[2,5,2,8,16]{4,3,2,1,0:T(8,128)}, u32[]{:S(2)}) copy-start(f32[2,5,2,8,16]{4,3,2,1,0:T(8,128)} %param.13) | copy-start | bytes 30724
  3.3 3.0 %collective-permute-start = (f32[64,128]{1,0:T(8,128)S(1)}, f32[64,128]{1,0:T(8,128)S(1)}, u32[]{:S(2)}, u32[]{:S(2)}) collective-permute-start(f32[64,128]{1,0:T(8,128)S(1)} %get-tuple-element.10), channel_id=1, source_target_pairs={{0,1},{1,0},{2,3},{3,2},{4,5},{5,4},{6,7},{7,6},{8,9},{9,8},{10,11... | collective-permute-start | bytes 98312 | tf_op jit(solution)/shard_map/ppermute | solution.py:416
  6.3 7.5 %collective-permute-start.1 = (f32[96,128]{1,0:T(8,128)S(1)}, f32[96,128]{1,0:T(8,128)S(1)}, u32[]{:S(2)}, u32[]{:S(2)}) collective-permute-start(f32[96,128]{1,0:T(8,128)S(1)} %get-tuple-element.12), channel_id=1, source_target_pairs={{0,2},{1,3},{2,0},{3,1},{4,6},{5,7},{6,4},{7,5},{8,10},{9,11},{10,... | collective-permute-start | bytes 147464 | tf_op jit(solution)/shard_map/ppermute | solution.py:427
  9.8 9.3 %collective-permute-start.2 = (f32[96,128]{1,0:T(8,128)S(1)}, f32[96,128]{1,0:T(8,128)S(1)}, u32[]{:S(2)}, u32[]{:S(2)}) collective-permute-start(f32[96,128]{1,0:T(8,128)S(1)} %get-tuple-element.13), channel_id=1, source_target_pairs={{4,66},{66,4},{5,67},{67,5},{8,70},{70,8},{9,71},{71,9},{12,74},{7... | collective-permute-start | bytes 147464 | tf_op jit(solution)/shard_map/ppermute | solution.py:426
  19.2 1.0 %copy-start.2 = (bf16[512,256]{1,0:T(8,128)(2,1)S(1)}, bf16[512,256]{1,0:T(8,128)(2,1)}, u32[]{:S(2)}) copy-start(bf16[512,256]{1,0:T(8,128)(2,1)} %merge_ref.1) | copy-start | bytes 786436
  20.1 0.9 %copy-start.3 = (bf16[256,512]{1,0:T(8,128)(2,1)S(1)}, bf16[256,512]{1,0:T(8,128)(2,1)}, u32[]{:S(2)}) copy-start(bf16[256,512]{1,0:T(8,128)(2,1)} %expand_ref.1) | copy-start | bytes 786436
  21.1 0.7 %copy-start.6 = (f32[7,256]{1,0:T(8,128)S(1)}, f32[7,256]{1,0:T(8,128)}, u32[]{:S(2)}) copy-start(f32[7,256]{1,0:T(8,128)} %embed_ref.1) | copy-start | bytes 21508
  21.8 0.7 %copy-start.8 = (bf16[128,5]{0,1:T(8,128)(2,1)S(1)}, bf16[128,5]{0,1:T(8,128)(2,1)}, u32[]{:S(2)}) copy-start(bf16[128,5]{0,1:T(8,128)(2,1)} %param.19) | copy-start | bytes 3844

commit v3 on v2

--- a/solution.py
+++ b/solution.py
@@ -13,7 +13,7 @@
 GROUP = 4
 VMEM_LIMIT = 50 * 1024 * 1024
 SMALL_LIMIT = 8 * 1024 * 1024
-R1 = 6
+R1 = 9
 RC = 1
 R2 = 4
 
@@ -40,10 +40,31 @@
     return segment ^ (2 * ((space // GROUP) % 2))
 
 
-def pack_kernel(state_ref, noise_ref, land_ref, own_ref, other_ref, even_ref, odd_ref):
+def pack_kernel(
+    state_hbm,
+    noise_hbm,
+    land_hbm,
+    own_ref,
+    other_ref,
+    state_ref,
+    noise_ref,
+    land_ref,
+    even_ref,
+    odd_ref,
+    sems,
+):
     member = member_of(lax.axis_index("segment"), lax.axis_index("space"))
+    copies = [
+        pltpu.make_async_copy(state_hbm, state_ref, sems.at[0]),
+        pltpu.make_async_copy(noise_hbm, noise_ref, sems.at[1]),
+        pltpu.make_async_copy(land_hbm, land_ref, sems.at[2]),
+    ]
+    for copy in copies:
+        copy.start()
     even_ref[...] = jnp.zeros_like(even_ref)
     odd_ref[...] = jnp.zeros_like(odd_ref)
+    for copy in copies:
+        copy.wait()
     for m in range(2):
         for lev in range(2):
             for y in range(8):
@@ -78,29 +99,36 @@
     far_ref[...] = jnp.where(upper, tail, head)
 
 
+def run_mask(v, row):
+    runs = v.reshape(v.shape[0] // 32, 32, v.shape[1])
+    return jnp.where(iota((1, 32, v.shape[1]), 1) != row, runs, 0.0).reshape(v.shape)
+
+
 def shift_down(v):
-    keep = iota(v.shape, 0) % 32 != 0
-    return jnp.where(keep, pltpu.roll(v, 1, 0), 0.0)
+    return run_mask(pltpu.roll(v, 1, 0), 0)
 
 
 def shift_up(v):
-    keep = iota(v.shape, 0) % 32 != 31
-    return jnp.where(keep, pltpu.roll(v, v.shape[0] - 1, 0), 0.0)
+    return run_mask(pltpu.roll(v, v.shape[0] - 1, 0), 31)
 
 
 def net_kernel(
     pair_ref,
     near_ref,
     far_ref,
-    embed_ref,
-    merge_ref,
-    expand_ref,
-    head_ref,
+    embed_hbm,
+    merge_hbm,
+    expand_hbm,
+    head_hbm,
     fine_hbm,
     coarse_hbm,
     out_ref,
     fine_w,
     coarse_w,
+    embed_ref,
+    merge_ref,
+    expand_ref,
+    head_ref,
     ew_ref,
     f_ref,
     ee,
@@ -124,7 +152,11 @@
     for k in range(4):
         copies.append(pltpu.make_async_copy(coarse_hbm.at[k], coarse_w.at[k], sems.at[1 + k]))
     copies.append(pltpu.make_async_copy(fine_hbm.at[1], fine_w.at[1], sems.at[5]))
-    for copy in copies:
+    merge_copy = pltpu.make_async_copy(merge_hbm, merge_ref, sems.at[6])
+    expand_copy = pltpu.make_async_copy(expand_hbm, expand_ref, sems.at[7])
+    head_copy = pltpu.make_async_copy(head_hbm, head_ref, sems.at[8])
+    embed_copy = pltpu.make_async_copy(embed_hbm, embed_ref, sems.at[9])
+    for copy in (embed_copy, copies[0], merge_copy, *copies[1:], expand_copy, head_copy):
         copy.start()
 
     near, far = near_ref[...], far_ref[...]
@@ -132,6 +164,7 @@
     f_ref[pl.ds(96, 128), :] = pair_ref[...]
     f_ref[pl.ds(224, 96), :] = jnp.where(upper, far, near)
 
+    embed_copy.wait()
     ew_ref[...] = jnp.zeros_like(ew_ref)
     ew_ref[pl.ds(0, 7), :] = embed_ref[...]
     w = ew_ref[...]
@@ -139,7 +172,7 @@
     w_lo = w - w_hi
     w4 = jnp.concatenate([w_hi, w_hi, w_lo, w_lo], axis=0).astype(BF16)
 
-    per = 4
+    per = 10
     def embed_block(i, _):
         for lev in range(2):
             parts = []
@@ -217,6 +250,7 @@
         dst[0, rows, lanes] = shift_down(v).astype(BF16)
         dst[2, rows, lanes] = shift_up(v).astype(BF16)
 
+    merge_copy.wait()
     for lev in range(2):
         lanes = pl.ds(lev * 256 + 128, 128)
         pieces = [
@@ -262,6 +296,7 @@
 
         src, dst = dst, src
 
+    expand_copy.wait()
     for lev in range(2):
         up = nn(src[1, pl.ds(0, 320), pl.ds(lev * 256, 256)], expand_ref[...])
         lanes = pl.ds(lev * 256, 128)
@@ -277,6 +312,7 @@
             ds1[rows, lanes] = down[here, odd].astype(BF16)
             ds2[rows, lanes] = high[here, even].astype(BF16)
 
+    head_copy.wait()
     row_id = iota((16, 5), 0)
     var_id = iota((16, 5), 1)
     head = jnp.concatenate(
@@ -287,11 +323,12 @@
         axis=1,
     ).astype(BF16)
 
-    src_lane = iota((512, 512), 0)
+    src_lane = iota((512, 1), 0)
     dst_lane = iota((512, 512), 1)
-    lon = 2 * (src_lane % 32) + src_lane // 256
-    lat = (src_lane // 32) % 8
-    spread = jnp.where(dst_lane == (lon // 16) * 128 + lat * 16 + lon % 16, 1.0, 0.0).astype(BF16)
+    lon = 2 * (src_lane & 31) + (src_lane >> 8)
+    lat = (src_lane >> 5) & 7
+    place = ((lon >> 4) << 7) + (lat << 4) + (lon & 15)
+    spread = jnp.where(dst_lane == place, 1.0, 0.0).astype(BF16)
 
     copies[5].wait()
     for half in range(2):
@@ -347,24 +384,28 @@
 def run_net(pair, near, far, embed_w, merge_w, expand_w, head_w, fine_weight_kernels, coarse_w):
     params = pltpu.CompilerParams(vmem_limit_bytes=VMEM_LIMIT)
     vmem = pl.BlockSpec(memory_space=pltpu.VMEM)
-    hbm = pl.BlockSpec(memory_space=pl.ANY)
+    hbm = pl.BlockSpec(memory_space=pltpu.HBM)
     e_buf = pltpu.VMEM((40 * 32, 512), BF16)
     d_buf = pltpu.VMEM((36 * 32, 512), BF16)
     increments = pl.pallas_call(
         net_kernel,
         out_shape=jax.ShapeDtypeStruct((8, 16, 128), F32),
-        in_specs=[vmem] * 7 + [hbm] * 2,
+        in_specs=[vmem] * 3 + [hbm] * 6,
         out_specs=vmem,
         scratch_shapes=[
             pltpu.VMEM((2, 6912, 128), BF16),
             pltpu.VMEM((4, 6912, 256), BF16),
+            pltpu.VMEM((7, 256), F32),
+            pltpu.VMEM((512, 256), BF16),
+            pltpu.VMEM((256, 512), BF16),
+            pltpu.VMEM((5, 128), BF16),
             pltpu.VMEM((8, 256), F32),
             pltpu.VMEM((320, 128), F32),
             *[e_buf] * 4,
             *[d_buf] * 4,
             pltpu.VMEM((3, 576, 512), BF16),
             pltpu.VMEM((3, 576, 512), BF16),
-            pltpu.SemaphoreType.DMA((6,)),
+            pltpu.SemaphoreType.DMA((10,)),
         ],
         compiler_params=params,
         name="net",
@@ -391,15 +432,23 @@
     columns = TILES // GROUP
     state_rows = state.reshape(160, 64)
     vmem = pl.BlockSpec(memory_space=pltpu.VMEM)
+    hbm = pl.BlockSpec(memory_space=pltpu.HBM)
 
     small = pltpu.CompilerParams(vmem_limit_bytes=SMALL_LIMIT)
     tile = jax.ShapeDtypeStruct((64, 128), F32)
     own, other = pl.pallas_call(
         pack_kernel,
         out_shape=(tile, tile),
-        in_specs=[vmem] * 3,
+        in_specs=[hbm] * 3,
         out_specs=(vmem, vmem),
-        scratch_shapes=[pltpu.VMEM((128, 64), F32), pltpu.VMEM((128, 64), F32)],
+        scratch_shapes=[
+            pltpu.VMEM((160, 64), F32),
+            pltpu.VMEM((2, 4, 2, 8, 64), F32),
+            pltpu.VMEM((8, 64), jnp.int32),
+            pltpu.VMEM((128, 64), F32),
+            pltpu.VMEM((128, 64), F32),
+            pltpu.SemaphoreType.DMA((3,)),
+        ],
         compiler_params=small,
         name="pack",
     )(state_rows, noise, land_sea)

time: 58.8 us -> 58.4 us (level)
    pallas_call x1, Pallas kernels: 24.9 us -> 24.2 us  [run_net(): pl.pallas_call(net_kernel, out_shape=jax.ShapeDtypeStruct((8, 16, 128), F...]
where the time goes in v3:
time: 58.4 us; the launch traced here: 58 us
  Pallas kernels  25.8 us (44%)
  blocking collectives  10 us (17%)
  starting transfers between devices  9.22 us (16%)
  waiting for transfers between devices  6.62 us (11%)
  local copies, waits for them, and re-layouts  5.69 us (10%)
  between operations  0.69 us (1%)
    pallas_call x1, Pallas kernels, run_net(): pl.pallas_call(net_kernel, out_shape=jax.ShapeDtypeStruct((8, 16, 128), F...  24.2 us
    all_to_all x1, blocking collectives, body(): lax.all_to_all(increments, AXES, 0, 0, axis_index_groups=squares, tiled=T...  10 us
    unnamed x18, local copies, waits for them, and re-layouts  5.69 us
    ppermute x1, waiting for transfers between devices, body(): far = lax.ppermute(far, AXES, beyond)  5.31 us
    ppermute x1, starting transfers between devices, body(): far = lax.ppermute(far, AXES, beyond)  4 us
    ppermute x1, starting transfers between devices, body(): near = lax.ppermute(near, AXES, across)  3.5 us
    ppermute x1, starting transfers between devices, body(): got = lax.ppermute(other, AXES, beside)  1.72 us
    ppermute x1, waiting for transfers between devices, body(): got = lax.ppermute(other, AXES, beside)  1.3 us
  transfers between devices with their start and end apart: 3, of which 2 were waited for; matrix products, arithmetic and copies ran while one was open for 0% of the time, Pallas kernels for 0%

profile of v3, /device:TPU:17, one launch (start us, length us, event | category | flops | bytes accessed | tf_op | source)
XLA Modules:
  0.0 58.0 jit_solution(14894433305863584133)
XLA Ops:
  0.6 0.0 copy-start
  0.6 0.9 %copy-done = f32[2,5,2,8,64]{4,3,2,1,0:T(8,128)S(1)} copy-done((f32[2,5,2,8,64]{4,3,2,1,0:T(8,128)S(1)}, f32[2,5,2,8,64]{4,3,2,1,0:T(8,128)}, u32[]{:S(2)}) %copy-start) | copy-done | bytes 40984
  1.5 0.0 copy-start.5
  1.5 0.8 %copy-done.5 = f32[2,4,2,8,64]{4,3,2,1,0:T(8,128)S(1)} copy-done((f32[2,4,2,8,64]{4,3,2,1,0:T(8,128)S(1)}, f32[2,4,2,8,64]{4,3,2,1,0:T(8,128)}, u32[]{:S(2)}) %copy-start.5) | copy-done | bytes 32792
  2.4 0.0 copy-start.7
  2.4 0.7 %copy-done.7 = s32[8,64]{1,0:T(8,128)S(1)} copy-done((s32[8,64]{1,0:T(8,128)S(1)}, s32[8,64]{1,0:T(8,128)}, u32[]{:S(2)}) %copy-start.7) | copy-done | bytes 2072
  3.0 0.0 copy-start.1
  3.0 0.0 copy-start.4
  3.0 0.5 pack.1
  3.5 1.7 %collective-permute-start = (f32[64,128]{1,0:T(8,128)S(1)}, f32[64,128]{1,0:T(8,128)S(1)}, u32[]{:S(2)}, u32[]{:S(2)}) collective-permute-start(f32[64,128]{1,0:T(8,128)S(1)} %get-tuple-element.10), channel_id=1, source_target_pairs={{0,1},{1,0},{2,3},{3,2},{4,5},{5,4},{6,7},{7,6},{8,9},{9,8},{10,11... | collective-permute-start | bytes 98312 | tf_op jit(solution)/shard_map/ppermute | solution.py:465
  5.2 1.3 %collective-permute-done.got_ref = f32[64,128]{1,0:T(8,128)S(1)} collective-permute-done((f32[64,128]{1,0:T(8,128)S(1)}, f32[64,128]{1,0:T(8,128)S(1)}, u32[]{:S(2)}, u32[]{:S(2)}) %collective-permute-start) | collective-permute-done | bytes 32800 | tf_op jit(solution)/shard_map/ppermute | solution.py:465
  6.6 3.5 %collective-permute-start.1 = (f32[96,128]{1,0:T(8,128)S(1)}, f32[96,128]{1,0:T(8,128)S(1)}, u32[]{:S(2)}, u32[]{:S(2)}) collective-permute-start(f32[96,128]{1,0:T(8,128)S(1)} %get-tuple-element.12), channel_id=1, source_target_pairs={{0,2},{1,3},{2,0},{3,1},{4,6},{5,7},{6,4},{7,5},{8,10},{9,11},{10,... | collective-permute-start | bytes 147464 | tf_op jit(solution)/shard_map/ppermute | solution.py:476
  10.1 4.0 %collective-permute-start.2 = (f32[96,128]{1,0:T(8,128)S(1)}, f32[96,128]{1,0:T(8,128)S(1)}, u32[]{:S(2)}, u32[]{:S(2)}) collective-permute-start(f32[96,128]{1,0:T(8,128)S(1)} %get-tuple-element.13), channel_id=1, source_target_pairs={{4,66},{66,4},{5,67},{67,5},{8,70},{70,8},{9,71},{71,9},{12,74},{7... | collective-permute-start | bytes 147464 | tf_op jit(solution)/shard_map/ppermute | solution.py:475
  14.1 0.0 collective-permute-done.1.near_ref
  14.1 5.3 %collective-permute-done.2.far_ref = f32[96,128]{1,0:T(8,128)S(1)} collective-permute-done((f32[96,128]{1,0:T(8,128)S(1)}, f32[96,128]{1,0:T(8,128)S(1)}, u32[]{:S(2)}, u32[]{:S(2)}) %collective-permute-start.2) | collective-permute-done | bytes 49184 | tf_op jit(solution)/shard_map/ppermute | solution.py:475
  19.4 0.9 %copy-done.2 = bf16[512,256]{1,0:T(8,128)(2,1)S(1)} copy-done((bf16[512,256]{1,0:T(8,128)(2,1)S(1)}, bf16[512,256]{1,0:T(8,128)(2,1)}, u32[]{:S(2)}) %copy-start.2) | copy-done | bytes 262168
  20.4 0.9 %copy-done.3 = bf16[256,512]{1,0:T(8,128)(2,1)S(1)} copy-done((bf16[256,512]{1,0:T(8,128)(2,1)S(1)}, bf16[256,512]{1,0:T(8,128)(2,1)}, u32[]{:S(2)}) %copy-start.3) | copy-done | bytes 262168
  21.3 0.7 %copy-done.6 = f32[7,256]{1,0:T(8,128)S(1)} copy-done((f32[7,256]{1,0:T(8,128)S(1)}, f32[7,256]{1,0:T(8,128)}, u32[]{:S(2)}) %copy-start.6) | copy-done | bytes 7192
  22.0 0.7 %copy-done.8 = bf16[128,5]{0,1:T(8,128)(2,1)S(1)} copy-done((bf16[128,5]{0,1:T(8,128)(2,1)S(1)}, bf16[128,5]{0,1:T(8,128)(2,1)}, u32[]{:S(2)}) %copy-start.8) | copy-done | bytes 1304
  22.7 24.2 %net.1 = f32[8,16,128]{2,1,0:T(8,128)S(1)} custom-call(f32[128,128]{1,0:T(8,128)S(1)} %get-tuple-element.11.pair_ref, f32[96,128]{1,0:T(8,128)S(1)} %collective-permute-done.1.near_ref, f32[96,128]{1,0:T(8,128)S(1)} %collective-permute-done.2.far_ref, f32[7,256]{1,0:T(8,128)S(1)} %copy-done.6, bf16[512,256]{1,0:T(8,128)(2,1)S(1)} %copy-done.2, ...), custom_call_target="tpu_custom_call" | custom-call | tf_op jit(solution)/shard_map/net/pallas_call | solution.py:390
  46.9 10.0 %all_to_all.5.got_ref = f32[8,16,128]{2,1,0:T(8,128)S(1)} all-to-all(f32[8,16,128]{2,1,0:T(8,128)S(1)} %net.1), channel_id=1, replica_groups={{0,1,32,33,64,65,96,97},{2,3,34,35,66,67,98,99},{4,5,36,37,68,69,100,10..., dimensions={0} | all-to-all | bytes 131072 | tf_op jit(solution)/shard_map/all_to_all | solution.py:486
  56.9 0.0 copy-done.1
  56.9 0.0 copy-done.4
  56.9 1.1 %score.1 = (f32[640,16]{1,0:T(8,128)}, f32[160,16]{1,0:T(8,128)}) custom-call(f32[8,16,128]{2,1,0:T(8,128)S(1)} %all_to_all.5.got_ref, f32[160,64]{1,0:T(8,128)S(1)} %bitcast.6, f32[160,16]{1,0:T(8,128)S(1)} %bitcast.7), custom_call_target="tpu_custom_call" | custom-call | tf_op jit(solution)/shard_map/score/pallas_call | solution.py:488
  (5 shorter events, 0.0 us)
Async XLA Ops:
  0.6 0.9 %copy-start = (f32[2,5,2,8,64]{4,3,2,1,0:T(8,128)S(1)}, f32[2,5,2,8,64]{4,3,2,1,0:T(8,128)}, u32[]{:S(2)}) copy-start(f32[2,5,2,8,64]{4,3,2,1,0:T(8,128)} %param.10) | copy-start | bytes 122884
  1.5 0.8 %copy-start.5 = (f32[2,4,2,8,64]{4,3,2,1,0:T(8,128)S(1)}, f32[2,4,2,8,64]{4,3,2,1,0:T(8,128)}, u32[]{:S(2)}) copy-start(f32[2,4,2,8,64]{4,3,2,1,0:T(8,128)} %noise_hbm.1) | copy-start | bytes 98308
  2.4 0.7 %copy-start.7 = (s32[8,64]{1,0:T(8,128)S(1)}, s32[8,64]{1,0:T(8,128)}, u32[]{:S(2)}) copy-start(s32[8,64]{1,0:T(8,128)} %land_hbm.1) | copy-start | bytes 6148
  3.0 53.8 %copy-start.1 = (f32[2,5,2,8,64]{4,3,2,1,0:T(8,128)S(1)}, f32[2,5,2,8,64]{4,3,2,1,0:T(8,128)}, u32[]{:S(2)}) copy-start(f32[2,5,2,8,64]{4,3,2,1,0:T(8,128)} %param.10) | copy-start | bytes 122884
  3.0 53.8 %copy-start.4 = (f32[2,5,2,8,16]{4,3,2,1,0:T(8,128)S(1)}, f32[2,5,2,8,16]{4,3,2,1,0:T(8,128)}, u32[]{:S(2)}) copy-start(f32[2,5,2,8,16]{4,3,2,1,0:T(8,128)} %param.13) | copy-start | bytes 30724
  3.5 3.0 %collective-permute-start = (f32[64,128]{1,0:T(8,128)S(1)}, f32[64,128]{1,0:T(8,128)S(1)}, u32[]{:S(2)}, u32[]{:S(2)}) collective-permute-start(f32[64,128]{1,0:T(8,128)S(1)} %get-tuple-element.10), channel_id=1, source_target_pairs={{0,1},{1,0},{2,3},{3,2},{4,5},{5,4},{6,7},{7,6},{8,9},{9,8},{10,11... | collective-permute-start | bytes 98312 | tf_op jit(solution)/shard_map/ppermute | solution.py:465
  6.6 7.5 %collective-permute-start.1 = (f32[96,128]{1,0:T(8,128)S(1)}, f32[96,128]{1,0:T(8,128)S(1)}, u32[]{:S(2)}, u32[]{:S(2)}) collective-permute-start(f32[96,128]{1,0:T(8,128)S(1)} %get-tuple-element.12), channel_id=1, source_target_pairs={{0,2},{1,3},{2,0},{3,1},{4,6},{5,7},{6,4},{7,5},{8,10},{9,11},{10,... | collective-permute-start | bytes 147464 | tf_op jit(solution)/shard_map/ppermute | solution.py:476
  10.1 9.3 %collective-permute-start.2 = (f32[96,128]{1,0:T(8,128)S(1)}, f32[96,128]{1,0:T(8,128)S(1)}, u32[]{:S(2)}, u32[]{:S(2)}) collective-permute-start(f32[96,128]{1,0:T(8,128)S(1)} %get-tuple-element.13), channel_id=1, source_target_pairs={{4,66},{66,4},{5,67},{67,5},{8,70},{70,8},{9,71},{71,9},{12,74},{7... | collective-permute-start | bytes 147464 | tf_op jit(solution)/shard_map/ppermute | solution.py:475
  19.4 1.0 %copy-start.2 = (bf16[512,256]{1,0:T(8,128)(2,1)S(1)}, bf16[512,256]{1,0:T(8,128)(2,1)}, u32[]{:S(2)}) copy-start(bf16[512,256]{1,0:T(8,128)(2,1)} %merge_hbm.1) | copy-start | bytes 786436
  20.3 0.9 %copy-start.3 = (bf16[256,512]{1,0:T(8,128)(2,1)S(1)}, bf16[256,512]{1,0:T(8,128)(2,1)}, u32[]{:S(2)}) copy-start(bf16[256,512]{1,0:T(8,128)(2,1)} %expand_hbm.1) | copy-start | bytes 786436
  21.3 0.7 %copy-start.6 = (f32[7,256]{1,0:T(8,128)S(1)}, f32[7,256]{1,0:T(8,128)}, u32[]{:S(2)}) copy-start(f32[7,256]{1,0:T(8,128)} %embed_hbm.1) | copy-start | bytes 21508
  22.0 0.7 %copy-start.8 = (bf16[128,5]{0,1:T(8,128)(2,1)S(1)}, bf16[128,5]{0,1:T(8,128)(2,1)}, u32[]{:S(2)}) copy-start(bf16[128,5]{0,1:T(8,128)(2,1)} %param.19) | copy-start | bytes 3844

commit v4 on v3

--- a/solution.py
+++ b/solution.py
@@ -13,6 +13,7 @@
 GROUP = 4
 VMEM_LIMIT = 50 * 1024 * 1024
 SMALL_LIMIT = 8 * 1024 * 1024
+PACK_LIMIT = 60 * 1024 * 1024
 R1 = 9
 RC = 1
 R2 = 4
@@ -99,6 +100,11 @@
     far_ref[...] = jnp.where(upper, tail, head)
 
 
+def fetch_kernel(_, *refs):
+    for src, dst in zip(refs[:4], refs[4:]):
+        dst[...] = src[...]
+
+
 def run_mask(v, row):
     runs = v.reshape(v.shape[0] // 32, 32, v.shape[1])
     return jnp.where(iota((1, 32, v.shape[1]), 1) != row, runs, 0.0).reshape(v.shape)
@@ -116,19 +122,15 @@
     pair_ref,
     near_ref,
     far_ref,
-    embed_hbm,
-    merge_hbm,
-    expand_hbm,
-    head_hbm,
+    embed_ref,
+    merge_ref,
+    expand_ref,
+    head_ref,
     fine_hbm,
     coarse_hbm,
     out_ref,
     fine_w,
     coarse_w,
-    embed_ref,
-    merge_ref,
-    expand_ref,
-    head_ref,
     ew_ref,
     f_ref,
     ee,
@@ -152,11 +154,7 @@
     for k in range(4):
         copies.append(pltpu.make_async_copy(coarse_hbm.at[k], coarse_w.at[k], sems.at[1 + k]))
     copies.append(pltpu.make_async_copy(fine_hbm.at[1], fine_w.at[1], sems.at[5]))
-    merge_copy = pltpu.make_async_copy(merge_hbm, merge_ref, sems.at[6])
-    expand_copy = pltpu.make_async_copy(expand_hbm, expand_ref, sems.at[7])
-    head_copy = pltpu.make_async_copy(head_hbm, head_ref, sems.at[8])
-    embed_copy = pltpu.make_async_copy(embed_hbm, embed_ref, sems.at[9])
-    for copy in (embed_copy, copies[0], merge_copy, *copies[1:], expand_copy, head_copy):
+    for copy in copies:
         copy.start()
 
     near, far = near_ref[...], far_ref[...]
@@ -164,7 +162,6 @@
     f_ref[pl.ds(96, 128), :] = pair_ref[...]
     f_ref[pl.ds(224, 96), :] = jnp.where(upper, far, near)
 
-    embed_copy.wait()
     ew_ref[...] = jnp.zeros_like(ew_ref)
     ew_ref[pl.ds(0, 7), :] = embed_ref[...]
     w = ew_ref[...]
@@ -250,7 +247,6 @@
         dst[0, rows, lanes] = shift_down(v).astype(BF16)
         dst[2, rows, lanes] = shift_up(v).astype(BF16)
 
-    merge_copy.wait()
     for lev in range(2):
         lanes = pl.ds(lev * 256 + 128, 128)
         pieces = [
@@ -296,7 +292,6 @@
 
         src, dst = dst, src
 
-    expand_copy.wait()
     for lev in range(2):
         up = nn(src[1, pl.ds(0, 320), pl.ds(lev * 256, 256)], expand_ref[...])
         lanes = pl.ds(lev * 256, 128)
@@ -312,7 +307,6 @@
             ds1[rows, lanes] = down[here, odd].astype(BF16)
             ds2[rows, lanes] = high[here, even].astype(BF16)
 
-    head_copy.wait()
     row_id = iota((16, 5), 0)
     var_id = iota((16, 5), 1)
     head = jnp.concatenate(
@@ -390,22 +384,18 @@
     increments = pl.pallas_call(
         net_kernel,
         out_shape=jax.ShapeDtypeStruct((8, 16, 128), F32),
-        in_specs=[vmem] * 3 + [hbm] * 6,
+        in_specs=[vmem] * 7 + [hbm] * 2,
         out_specs=vmem,
         scratch_shapes=[
             pltpu.VMEM((2, 6912, 128), BF16),
             pltpu.VMEM((4, 6912, 256), BF16),
-            pltpu.VMEM((7, 256), F32),
-            pltpu.VMEM((512, 256), BF16),
-            pltpu.VMEM((256, 512), BF16),
-            pltpu.VMEM((5, 128), BF16),
             pltpu.VMEM((8, 256), F32),
             pltpu.VMEM((320, 128), F32),
             *[e_buf] * 4,
             *[d_buf] * 4,
             pltpu.VMEM((3, 576, 512), BF16),
             pltpu.VMEM((3, 576, 512), BF16),
-            pltpu.SemaphoreType.DMA((10,)),
+            pltpu.SemaphoreType.DMA((6,)),
         ],
         compiler_params=params,
         name="net",
@@ -449,7 +439,7 @@
             pltpu.VMEM((128, 64), F32),
             pltpu.SemaphoreType.DMA((3,)),
         ],
-        compiler_params=small,
+        compiler_params=pltpu.CompilerParams(vmem_limit_bytes=PACK_LIMIT),
         name="pack",
     )(state_rows, noise, land_sea)
 
@@ -472,10 +462,20 @@
         compiler_params=small,
         name="join",
     )(own, got)
+    weights = (embed_w, merge_w, expand_w, head_w.T)
+    embed_w, merge_w, expand_w, head_w = pl.pallas_call(
+        fetch_kernel,
+        out_shape=tuple(jax.ShapeDtypeStruct(w.shape, w.dtype) for w in weights),
+        in_specs=[pl.BlockSpec(memory_space=pl.ANY)] + [vmem] * 4,
+        out_specs=(vmem,) * 4,
+        compiler_params=small,
+        cost_estimate=pl.CostEstimate(flops=0, bytes_accessed=1 << 22, transcendentals=0),
+        name="fetch",
+    )(pair, *weights)
     far = lax.ppermute(far, AXES, beyond)
     near = lax.ppermute(near, AXES, across)
     increments = run_net(
-        pair, near, far, embed_w, merge_w, expand_w, head_w.T, fine_weight_kernels, coarse_w
+        pair, near, far, embed_w, merge_w, expand_w, head_w, fine_weight_kernels, coarse_w
     )
 
     squares = [

time: 58.4 us -> 55 us (0.942)
  waiting for transfers between devices: 6.62 us -> 3.51 us
  local copies, waits for them, and re-layouts: 5.69 us -> 4.04 us
  Pallas kernels: 25.8 us -> 27.2 us
    ppermute x1, waiting for transfers between devices: 5.31 us -> 1.99 us  [body(): far = lax.ppermute(far, AXES, beyond)]
    unnamed x18 -> x14, local copies, waits for them, and re-layouts: 5.69 us -> 4.04 us
    pallas_call x1, Pallas kernels: 0.46 us -> 1.84 us  [body(): pl.pallas_call(pack_kernel, out_shape=(tile, tile), in_specs=[hbm] * 3, o...]
where the time goes in v4:
time: 55 us; the launch traced here: 54.6 us
  Pallas kernels  27.2 us (49%)
  blocking collectives  9.99 us (18%)
  starting transfers between devices  9.22 us (17%)
  local copies, waits for them, and re-layouts  4.04 us (7%)
  waiting for transfers between devices  3.51 us (6%)
  between operations  0.7 us (1%)
    pallas_call x1, Pallas kernels, run_net(): pl.pallas_call(net_kernel, out_shape=jax.ShapeDtypeStruct((8, 16, 128), F...  24.2 us
    all_to_all x1, blocking collectives, body(): lax.all_to_all(increments, AXES, 0, 0, axis_index_groups=squares, tiled=T...  9.99 us
    unnamed x14, local copies, waits for them, and re-layouts  4.04 us
    ppermute x1, starting transfers between devices, body(): far = lax.ppermute(far, AXES, beyond)  4 us
    ppermute x1, starting transfers between devices, body(): near = lax.ppermute(near, AXES, across)  3.5 us
    ppermute x1, waiting for transfers between devices, body(): far = lax.ppermute(far, AXES, beyond)  1.99 us
    pallas_call x1, Pallas kernels, body(): pl.pallas_call(pack_kernel, out_shape=(tile, tile), in_specs=[hbm] * 3, o...  1.84 us
    ppermute x1, starting transfers between devices, body(): got = lax.ppermute(other, AXES, beside)  1.72 us
  transfers between devices with their start and end apart: 3, of which 2 were waited for; matrix products, arithmetic and copies ran while one was open for 0% of the time, Pallas kernels for 0%

profile of v4, /device:TPU:17, one launch (start us, length us, event | category | flops | bytes accessed | tf_op | source)
XLA Modules:
  0.0 54.6 jit_solution(15202541077412490811)
XLA Ops:
  0.6 0.0 copy-start
  0.6 0.0 copy-start.3
  0.7 1.8 %pack.1 = (f32[64,128]{1,0:T(8,128)}, f32[64,128]{1,0:T(8,128)}) custom-call(f32[160,64]{1,0:T(8,128)} %bitcast.5, f32[2,4,2,8,64]{4,3,2,1,0:T(8,128)} %noise_hbm.1, s32[8,64]{1,0:T(8,128)} %land_hbm.1), custom_call_target="tpu_custom_call" | custom-call | tf_op jit(solution)/shard_map/pack/pallas_call | solution.py:429
  2.5 1.7 %collective-permute-start = (f32[64,128]{1,0:T(8,128)}, f32[64,128]{1,0:T(8,128)S(1)}, u32[]{:S(2)}, u32[]{:S(2)}) collective-permute-start(f32[64,128]{1,0:T(8,128)} %get-tuple-element.14), channel_id=1, source_target_pairs={{0,1},{1,0},{2,3},{3,2},{4,5},{5,4},{6,7},{7,6},{8,9},{9,8},{10,11... | collective-permute-start | bytes 98312 | tf_op jit(solution)/shard_map/ppermute | solution.py:455
  4.2 1.5 %collective-permute-done.got_ref = f32[64,128]{1,0:T(8,128)S(1)} collective-permute-done((f32[64,128]{1,0:T(8,128)}, f32[64,128]{1,0:T(8,128)S(1)}, u32[]{:S(2)}, u32[]{:S(2)}) %collective-permute-start) | collective-permute-done | bytes 32800 | tf_op jit(solution)/shard_map/ppermute | solution.py:455
  5.7 0.0 copy-start.4
  5.7 0.8 %copy-done.4 = f32[64,128]{1,0:T(8,128)S(1)} copy-done((f32[64,128]{1,0:T(8,128)S(1)}, f32[64,128]{1,0:T(8,128)}, u32[]{:S(2)}) %copy-start.4) | copy-done | bytes 32792
  6.5 3.5 %collective-permute-start.1 = (f32[96,128]{1,0:T(8,128)S(1)}, f32[96,128]{1,0:T(8,128)S(1)}, u32[]{:S(2)}, u32[]{:S(2)}) collective-permute-start(f32[96,128]{1,0:T(8,128)S(1)} %get-tuple-element.16), channel_id=1, source_target_pairs={{0,2},{1,3},{2,0},{3,1},{4,6},{5,7},{6,4},{7,5},{8,10},{9,11},{10,... | collective-permute-start | bytes 147464 | tf_op jit(solution)/shard_map/ppermute | solution.py:476
  10.0 4.0 %collective-permute-start.2 = (f32[96,128]{1,0:T(8,128)S(1)}, f32[96,128]{1,0:T(8,128)S(1)}, u32[]{:S(2)}, u32[]{:S(2)}) collective-permute-start(f32[96,128]{1,0:T(8,128)S(1)} %get-tuple-element.17), channel_id=1, source_target_pairs={{4,66},{66,4},{5,67},{67,5},{8,70},{70,8},{9,71},{71,9},{12,74},{7... | collective-permute-start | bytes 147464 | tf_op jit(solution)/shard_map/ppermute | solution.py:475
  14.0 0.0 copy-start.1
  14.0 0.9 %copy-done.1 = bf16[512,256]{1,0:T(8,128)(2,1)S(1)} copy-done((bf16[512,256]{1,0:T(8,128)(2,1)S(1)}, bf16[512,256]{1,0:T(8,128)(2,1)}, u32[]{:S(2)}) %copy-start.1) | copy-done | bytes 262168
  15.0 0.0 copy-start.2
  15.0 0.9 %copy-done.2 = bf16[256,512]{1,0:T(8,128)(2,1)S(1)} copy-done((bf16[256,512]{1,0:T(8,128)(2,1)S(1)}, bf16[256,512]{1,0:T(8,128)(2,1)}, u32[]{:S(2)}) %copy-start.2) | copy-done | bytes 262168
  15.9 0.0 copy-start.5
  15.9 0.7 %copy-done.5 = f32[7,256]{1,0:T(8,128)S(1)} copy-done((f32[7,256]{1,0:T(8,128)S(1)}, f32[7,256]{1,0:T(8,128)}, u32[]{:S(2)}) %copy-start.5) | copy-done | bytes 7192
  16.6 0.0 copy-start.6
  16.6 0.7 %copy-done.6 = bf16[128,5]{0,1:T(8,128)(2,1)S(1)} copy-done((bf16[128,5]{0,1:T(8,128)(2,1)S(1)}, bf16[128,5]{0,1:T(8,128)(2,1)}, u32[]{:S(2)}) %copy-start.6) | copy-done | bytes 1304
  17.3 0.0 collective-permute-done.1.near_ref
  17.4 2.0 %collective-permute-done.2.far_ref = f32[96,128]{1,0:T(8,128)S(1)} collective-permute-done((f32[96,128]{1,0:T(8,128)S(1)}, f32[96,128]{1,0:T(8,128)S(1)}, u32[]{:S(2)}, u32[]{:S(2)}) %collective-permute-start.2) | collective-permute-done | bytes 49184 | tf_op jit(solution)/shard_map/ppermute | solution.py:475
  19.3 24.2 %net.1 = f32[8,16,128]{2,1,0:T(8,128)S(1)} custom-call(f32[128,128]{1,0:T(8,128)S(1)} %get-tuple-element.15._.pair_ref, f32[96,128]{1,0:T(8,128)S(1)} %collective-permute-done.1.near_ref, f32[96,128]{1,0:T(8,128)S(1)} %collective-permute-done.2.far_ref, f32[7,256]{1,0:T(8,128)S(1)} %get-tuple-element.18.embed_ref, ...), custom_call_target="tpu_custom_call" | custom-call | tf_op jit(solution)/shard_map/net/pallas_call | solution.py:384
  43.5 10.0 %all_to_all.5.got_ref = f32[8,16,128]{2,1,0:T(8,128)S(1)} all-to-all(f32[8,16,128]{2,1,0:T(8,128)S(1)} %net.1), channel_id=1, replica_groups={{0,1,32,33,64,65,96,97},{2,3,34,35,66,67,98,99},{4,5,36,37,68,69,100,10..., dimensions={0} | all-to-all | bytes 131072 | tf_op jit(solution)/shard_map/all_to_all | solution.py:486
  53.5 0.0 copy-done
  53.5 0.0 copy-done.3
  53.5 1.1 %score.1 = (f32[640,16]{1,0:T(8,128)}, f32[160,16]{1,0:T(8,128)}) custom-call(f32[8,16,128]{2,1,0:T(8,128)S(1)} %all_to_all.5.got_ref, f32[160,64]{1,0:T(8,128)S(1)} %bitcast.6, f32[160,16]{1,0:T(8,128)S(1)} %bitcast.7), custom_call_target="tpu_custom_call" | custom-call | tf_op jit(solution)/shard_map/score/pallas_call | solution.py:488
  (2 shorter events, 0.1 us)
Async XLA Ops:
  0.6 52.9 %copy-start = (f32[2,5,2,8,64]{4,3,2,1,0:T(8,128)S(1)}, f32[2,5,2,8,64]{4,3,2,1,0:T(8,128)}, u32[]{:S(2)}) copy-start(f32[2,5,2,8,64]{4,3,2,1,0:T(8,128)} %param.10) | copy-start | bytes 122884
  0.6 52.9 %copy-start.3 = (f32[2,5,2,8,16]{4,3,2,1,0:T(8,128)S(1)}, f32[2,5,2,8,16]{4,3,2,1,0:T(8,128)}, u32[]{:S(2)}) copy-start(f32[2,5,2,8,16]{4,3,2,1,0:T(8,128)} %param.13) | copy-start | bytes 30724
  2.5 3.2 %collective-permute-start = (f32[64,128]{1,0:T(8,128)}, f32[64,128]{1,0:T(8,128)S(1)}, u32[]{:S(2)}, u32[]{:S(2)}) collective-permute-start(f32[64,128]{1,0:T(8,128)} %get-tuple-element.14), channel_id=1, source_target_pairs={{0,1},{1,0},{2,3},{3,2},{4,5},{5,4},{6,7},{7,6},{8,9},{9,8},{10,11... | collective-permute-start | bytes 98312 | tf_op jit(solution)/shard_map/ppermute | solution.py:455
  5.7 0.8 %copy-start.4 = (f32[64,128]{1,0:T(8,128)S(1)}, f32[64,128]{1,0:T(8,128)}, u32[]{:S(2)}) copy-start(f32[64,128]{1,0:T(8,128)} %get-tuple-element.13.own_ref) | copy-start | bytes 98308
  6.5 10.8 %collective-permute-start.1 = (f32[96,128]{1,0:T(8,128)S(1)}, f32[96,128]{1,0:T(8,128)S(1)}, u32[]{:S(2)}, u32[]{:S(2)}) collective-permute-start(f32[96,128]{1,0:T(8,128)S(1)} %get-tuple-element.16), channel_id=1, source_target_pairs={{0,2},{1,3},{2,0},{3,1},{4,6},{5,7},{6,4},{7,5},{8,10},{9,11},{10,... | collective-permute-start | bytes 147464 | tf_op jit(solution)/shard_map/ppermute | solution.py:476
  10.0 9.3 %collective-permute-start.2 = (f32[96,128]{1,0:T(8,128)S(1)}, f32[96,128]{1,0:T(8,128)S(1)}, u32[]{:S(2)}, u32[]{:S(2)}) collective-permute-start(f32[96,128]{1,0:T(8,128)S(1)} %get-tuple-element.17), channel_id=1, source_target_pairs={{4,66},{66,4},{5,67},{67,5},{8,70},{70,8},{9,71},{71,9},{12,74},{7... | collective-permute-start | bytes 147464 | tf_op jit(solution)/shard_map/ppermute | solution.py:475
  14.0 1.0 %copy-start.1 = (bf16[512,256]{1,0:T(8,128)(2,1)S(1)}, bf16[512,256]{1,0:T(8,128)(2,1)}, u32[]{:S(2)}) copy-start(bf16[512,256]{1,0:T(8,128)(2,1)} %refs_1_.1) | copy-start | bytes 786436
  15.0 0.9 %copy-start.2 = (bf16[256,512]{1,0:T(8,128)(2,1)S(1)}, bf16[256,512]{1,0:T(8,128)(2,1)}, u32[]{:S(2)}) copy-start(bf16[256,512]{1,0:T(8,128)(2,1)} %refs_2_.1) | copy-start | bytes 786436
  15.9 0.7 %copy-start.5 = (f32[7,256]{1,0:T(8,128)S(1)}, f32[7,256]{1,0:T(8,128)}, u32[]{:S(2)}) copy-start(f32[7,256]{1,0:T(8,128)} %refs_0_.1) | copy-start | bytes 21508
  16.6 0.7 %copy-start.6 = (bf16[128,5]{0,1:T(8,128)(2,1)S(1)}, bf16[128,5]{0,1:T(8,128)(2,1)}, u32[]{:S(2)}) copy-start(bf16[128,5]{0,1:T(8,128)(2,1)} %param.19) | copy-start | bytes 3844

commit v5 on v4

--- a/solution.py
+++ b/solution.py
@@ -100,9 +100,43 @@
     far_ref[...] = jnp.where(upper, tail, head)
 
 
-def fetch_kernel(_, *refs):
-    for src, dst in zip(refs[:4], refs[4:]):
-        dst[...] = src[...]
+def fetch_kernel(
+    _,
+    embed_ref,
+    merge_in,
+    expand_in,
+    head_ref,
+    w4_ref,
+    merge_out,
+    expand_out,
+    row_ref,
+    spread_ref,
+    ew_ref,
+):
+    merge_out[...] = merge_in[...]
+    expand_out[...] = expand_in[...]
+    ew_ref[...] = jnp.zeros_like(ew_ref)
+    ew_ref[pl.ds(0, 7), :] = embed_ref[...]
+    w = ew_ref[...]
+    w_hi = w.astype(BF16).astype(F32)
+    w_lo = w - w_hi
+    w4_ref[...] = jnp.concatenate([w_hi, w_hi, w_lo, w_lo], axis=0).astype(BF16)
+    row_id = iota((16, 5), 0)
+    var_id = iota((16, 5), 1)
+    row_ref[...] = jnp.concatenate(
+        [
+            nn(jnp.where(row_id == 2 * var_id + lev, 1.0, 0.0).astype(BF16), head_ref[...])
+            for lev in range(2)
+        ],
+        axis=1,
+    ).astype(BF16)
+
+    src_lane = iota((512, 1), 0)
+    dst_lane = iota((512, 512), 1)
+    lon = 2 * (src_lane & 31) + (src_lane >> 8)
+    lat = (src_lane >> 5) & 7
+    place = ((lon >> 4) << 7) + (lat << 4) + (lon & 15)
+    spread_ref[...] = jnp.where(dst_lane == place, 1.0, 0.0).astype(BF16)
 
 
 def run_mask(v, row):
@@ -126,12 +160,12 @@
     merge_ref,
     expand_ref,
     head_ref,
+    spread_ref,
     fine_hbm,
     coarse_hbm,
     out_ref,
     fine_w,
     coarse_w,
-    ew_ref,
     f_ref,
     ee,
     eo,
@@ -162,13 +196,7 @@
     f_ref[pl.ds(96, 128), :] = pair_ref[...]
     f_ref[pl.ds(224, 96), :] = jnp.where(upper, far, near)
 
-    ew_ref[...] = jnp.zeros_like(ew_ref)
-    ew_ref[pl.ds(0, 7), :] = embed_ref[...]
-    w = ew_ref[...]
-    w_hi = w.astype(BF16).astype(F32)
-    w_lo = w - w_hi
-    w4 = jnp.concatenate([w_hi, w_hi, w_lo, w_lo], axis=0).astype(BF16)
-
+    w4 = embed_ref[...]
     per = 10
     def embed_block(i, _):
         for lev in range(2):
@@ -307,23 +335,7 @@
             ds1[rows, lanes] = down[here, odd].astype(BF16)
             ds2[rows, lanes] = high[here, even].astype(BF16)
 
-    row_id = iota((16, 5), 0)
-    var_id = iota((16, 5), 1)
-    head = jnp.concatenate(
-        [
-            nn(jnp.where(row_id == 2 * var_id + lev, 1.0, 0.0).astype(BF16), head_ref[...])
-            for lev in range(2)
-        ],
-        axis=1,
-    ).astype(BF16)
-
-    src_lane = iota((512, 1), 0)
-    dst_lane = iota((512, 512), 1)
-    lon = 2 * (src_lane & 31) + (src_lane >> 8)
-    lat = (src_lane >> 5) & 7
-    place = ((lon >> 4) << 7) + (lat << 4) + (lon & 15)
-    spread = jnp.where(dst_lane == place, 1.0, 0.0).astype(BF16)
-
+    head, spread = head_ref[...], spread_ref[...]
     copies[5].wait()
     for half in range(2):
         evens, odds = [], []
@@ -375,7 +387,7 @@
         put(crps_ref, m * 80, skill - spread * (1.0 / 12.0))
 
 
-def run_net(pair, near, far, embed_w, merge_w, expand_w, head_w, fine_weight_kernels, coarse_w):
+def run_net(pair, near, far, w4, merge_w, expand_w, head, spread, fine_weight_kernels, coarse_w):
     params = pltpu.CompilerParams(vmem_limit_bytes=VMEM_LIMIT)
     vmem = pl.BlockSpec(memory_space=pltpu.VMEM)
     hbm = pl.BlockSpec(memory_space=pltpu.HBM)
@@ -384,12 +396,11 @@
     increments = pl.pallas_call(
         net_kernel,
         out_shape=jax.ShapeDtypeStruct((8, 16, 128), F32),
-        in_specs=[vmem] * 7 + [hbm] * 2,
+        in_specs=[vmem] * 8 + [hbm] * 2,
         out_specs=vmem,
         scratch_shapes=[
             pltpu.VMEM((2, 6912, 128), BF16),
             pltpu.VMEM((4, 6912, 256), BF16),
-            pltpu.VMEM((8, 256), F32),
             pltpu.VMEM((320, 128), F32),
             *[e_buf] * 4,
             *[d_buf] * 4,
@@ -399,7 +410,7 @@
         ],
         compiler_params=params,
         name="net",
-    )(pair, near, far, embed_w, merge_w, expand_w, head_w, fine_weight_kernels, coarse_w)
+    )(pair, near, far, w4, merge_w, expand_w, head, spread, fine_weight_kernels, coarse_w)
     return increments
 
 
@@ -462,20 +473,21 @@
         compiler_params=small,
         name="join",
     )(own, got)
-    weights = (embed_w, merge_w, expand_w, head_w.T)
-    embed_w, merge_w, expand_w, head_w = pl.pallas_call(
+    made = ((32, 256), merge_w.shape, expand_w.shape, (16, 256), (512, 512))
+    w4, merge_w, expand_w, head, spread = pl.pallas_call(
         fetch_kernel,
-        out_shape=tuple(jax.ShapeDtypeStruct(w.shape, w.dtype) for w in weights),
+        out_shape=tuple(jax.ShapeDtypeStruct(shape, BF16) for shape in made),
         in_specs=[pl.BlockSpec(memory_space=pl.ANY)] + [vmem] * 4,
-        out_specs=(vmem,) * 4,
+        out_specs=(vmem,) * 5,
+        scratch_shapes=[pltpu.VMEM((8, 256), F32)],
         compiler_params=small,
         cost_estimate=pl.CostEstimate(flops=0, bytes_accessed=1 << 22, transcendentals=0),
         name="fetch",
-    )(pair, *weights)
+    )(pair, embed_w, merge_w, expand_w, head_w.T)
     far = lax.ppermute(far, AXES, beyond)
     near = lax.ppermute(near, AXES, across)
     increments = run_net(
-        pair, near, far, embed_w, merge_w, expand_w, head_w, fine_weight_kernels, coarse_w
+        pair, near, far, w4, merge_w, expand_w, head, spread, fine_weight_kernels, coarse_w
     )
 
     squares = [

time: 55 us -> 54.8 us (level)
  transfers between devices with their start and end apart: 3 -> 3, of which waited for: 2 -> 2; matrix products, arithmetic and copies ran while one was open for 0% -> 0% of each run, Pallas kernels for 0% -> 1%
where the time goes in v5:
time: 54.8 us; the launch traced here: 54.4 us
  Pallas kernels  27.3 us (50%)
  blocking collectives  9.99 us (18%)
  starting transfers between devices  9.22 us (17%)
  local copies, waits for them, and re-layouts  4.04 us (7%)
  waiting for transfers between devices  3.12 us (6%)
  between operations  0.7 us (1%)
    pallas_call x1, Pallas kernels, run_net(): pl.pallas_call(net_kernel, out_shape=jax.ShapeDtypeStruct((8, 16, 128), F...  23.9 us
    all_to_all x1, blocking collectives, body(): lax.all_to_all(increments, AXES, 0, 0, axis_index_groups=squares, tiled=T...  9.99 us
    unnamed x14, local copies, waits for them, and re-layouts  4.04 us
    ppermute x1, starting transfers between devices, body(): far = lax.ppermute(far, AXES, beyond)  4 us
    ppermute x1, starting transfers between devices, body(): near = lax.ppermute(near, AXES, across)  3.5 us
    pallas_call x1, Pallas kernels, body(): pl.pallas_call(pack_kernel, out_shape=(tile, tile), in_specs=[hbm] * 3, o...  1.84 us
    ppermute x1, starting transfers between devices, body(): got = lax.ppermute(other, AXES, beside)  1.72 us
    ppermute x1, waiting for transfers between devices, body(): far = lax.ppermute(far, AXES, beyond)  1.6 us
  transfers between devices with their start and end apart: 3, of which 2 were waited for; matrix products, arithmetic and copies ran while one was open for 0% of the time, Pallas kernels for 1%

profile of v5, /device:TPU:17, one launch (start us, length us, event | category | flops | bytes accessed | tf_op | source)
XLA Modules:
  0.0 54.4 jit_solution(6728465288648533429)
XLA Ops:
  0.6 0.0 copy-start
  0.6 0.0 copy-start.3
  0.7 1.8 %pack.1 = (f32[64,128]{1,0:T(8,128)}, f32[64,128]{1,0:T(8,128)}) custom-call(f32[160,64]{1,0:T(8,128)} %bitcast.5, f32[2,4,2,8,64]{4,3,2,1,0:T(8,128)} %noise_hbm.1, s32[8,64]{1,0:T(8,128)} %land_hbm.1), custom_call_target="tpu_custom_call" | custom-call | tf_op jit(solution)/shard_map/pack/pallas_call | solution.py:440
  2.5 1.7 %collective-permute-start = (f32[64,128]{1,0:T(8,128)}, f32[64,128]{1,0:T(8,128)S(1)}, u32[]{:S(2)}, u32[]{:S(2)}) collective-permute-start(f32[64,128]{1,0:T(8,128)} %get-tuple-element.15), channel_id=1, source_target_pairs={{0,1},{1,0},{2,3},{3,2},{4,5},{5,4},{6,7},{7,6},{8,9},{9,8},{10,11... | collective-permute-start | bytes 98312 | tf_op jit(solution)/shard_map/ppermute | solution.py:466
  4.2 1.5 %collective-permute-done.got_ref = f32[64,128]{1,0:T(8,128)S(1)} collective-permute-done((f32[64,128]{1,0:T(8,128)}, f32[64,128]{1,0:T(8,128)S(1)}, u32[]{:S(2)}, u32[]{:S(2)}) %collective-permute-start) | collective-permute-done | bytes 32800 | tf_op jit(solution)/shard_map/ppermute | solution.py:466
  5.7 0.0 copy-start.4
  5.7 0.8 %copy-done.4 = f32[64,128]{1,0:T(8,128)S(1)} copy-done((f32[64,128]{1,0:T(8,128)S(1)}, f32[64,128]{1,0:T(8,128)}, u32[]{:S(2)}) %copy-start.4) | copy-done | bytes 32792
  6.5 3.5 %collective-permute-start.1 = (f32[96,128]{1,0:T(8,128)S(1)}, f32[96,128]{1,0:T(8,128)S(1)}, u32[]{:S(2)}, u32[]{:S(2)}) collective-permute-start(f32[96,128]{1,0:T(8,128)S(1)} %get-tuple-element.17), channel_id=1, source_target_pairs={{0,2},{1,3},{2,0},{3,1},{4,6},{5,7},{6,4},{7,5},{8,10},{9,11},{10,... | collective-permute-start | bytes 147464 | tf_op jit(solution)/shard_map/ppermute | solution.py:488
  10.0 4.0 %collective-permute-start.2 = (f32[96,128]{1,0:T(8,128)S(1)}, f32[96,128]{1,0:T(8,128)S(1)}, u32[]{:S(2)}, u32[]{:S(2)}) collective-permute-start(f32[96,128]{1,0:T(8,128)S(1)} %get-tuple-element.18), channel_id=1, source_target_pairs={{4,66},{66,4},{5,67},{67,5},{8,70},{70,8},{9,71},{71,9},{12,74},{7... | collective-permute-start | bytes 147464 | tf_op jit(solution)/shard_map/ppermute | solution.py:487
  14.0 0.0 copy-start.1
  14.0 0.9 %copy-done.1 = bf16[512,256]{1,0:T(8,128)(2,1)S(1)} copy-done((bf16[512,256]{1,0:T(8,128)(2,1)S(1)}, bf16[512,256]{1,0:T(8,128)(2,1)}, u32[]{:S(2)}) %copy-start.1) | copy-done | bytes 262168
  15.0 0.0 copy-start.2
  15.0 0.9 %copy-done.2 = bf16[256,512]{1,0:T(8,128)(2,1)S(1)} copy-done((bf16[256,512]{1,0:T(8,128)(2,1)S(1)}, bf16[256,512]{1,0:T(8,128)(2,1)}, u32[]{:S(2)}) %copy-start.2) | copy-done | bytes 262168
  15.9 0.0 copy-start.5
  15.9 0.7 %copy-done.5 = f32[7,256]{1,0:T(8,128)S(1)} copy-done((f32[7,256]{1,0:T(8,128)S(1)}, f32[7,256]{1,0:T(8,128)}, u32[]{:S(2)}) %copy-start.5) | copy-done | bytes 7192
  16.6 0.7 %copy-done.6 = bf16[128,5]{0,1:T(8,128)(2,1)S(1)} copy-done((bf16[128,5]{0,1:T(8,128)(2,1)S(1)}, bf16[128,5]{0,1:T(8,128)(2,1)}, u32[]{:S(2)}) %copy-start.6) | copy-done | bytes 1304
  17.3 0.4 fetch.1
  17.7 0.0 collective-permute-done.1.near_ref
  17.7 1.6 %collective-permute-done.2.far_ref = f32[96,128]{1,0:T(8,128)S(1)} collective-permute-done((f32[96,128]{1,0:T(8,128)S(1)}, f32[96,128]{1,0:T(8,128)S(1)}, u32[]{:S(2)}, u32[]{:S(2)}) %collective-permute-start.2) | collective-permute-done | bytes 49184 | tf_op jit(solution)/shard_map/ppermute | solution.py:487
  19.3 23.9 %net.1 = f32[8,16,128]{2,1,0:T(8,128)S(1)} custom-call(f32[128,128]{1,0:T(8,128)S(1)} %get-tuple-element.16._.pair_ref, f32[96,128]{1,0:T(8,128)S(1)} %collective-permute-done.1.near_ref, f32[96,128]{1,0:T(8,128)S(1)} %collective-permute-done.2.far_ref, bf16[32,256]{1,0:T(8,128)(2,1)S(1)} %get-tuple-element.19.embed_ref, ...), custom_call_target="tpu_custom_call" | custom-call | tf_op jit(solution)/shard_map/net/pallas_call | solution.py:396
  43.3 10.0 %all_to_all.5.got_ref = f32[8,16,128]{2,1,0:T(8,128)S(1)} all-to-all(f32[8,16,128]{2,1,0:T(8,128)S(1)} %net.1), channel_id=1, replica_groups={{0,1,32,33,64,65,96,97},{2,3,34,35,66,67,98,99},{4,5,36,37,68,69,100,10..., dimensions={0} | all-to-all | bytes 131072 | tf_op jit(solution)/shard_map/all_to_all | solution.py:498
  53.2 0.0 copy-done
  53.2 0.0 copy-done.3
  53.3 1.1 %score.1 = (f32[640,16]{1,0:T(8,128)}, f32[160,16]{1,0:T(8,128)}) custom-call(f32[8,16,128]{2,1,0:T(8,128)S(1)} %all_to_all.5.got_ref, f32[160,64]{1,0:T(8,128)S(1)} %bitcast.6, f32[160,16]{1,0:T(8,128)S(1)} %bitcast.7), custom_call_target="tpu_custom_call" | custom-call | tf_op jit(solution)/shard_map/score/pallas_call | solution.py:500
  (2 shorter events, 0.0 us)
Async XLA Ops:
  0.6 52.6 %copy-start = (f32[2,5,2,8,64]{4,3,2,1,0:T(8,128)S(1)}, f32[2,5,2,8,64]{4,3,2,1,0:T(8,128)}, u32[]{:S(2)}) copy-start(f32[2,5,2,8,64]{4,3,2,1,0:T(8,128)} %param.10) | copy-start | bytes 122884
  0.6 52.6 %copy-start.3 = (f32[2,5,2,8,16]{4,3,2,1,0:T(8,128)S(1)}, f32[2,5,2,8,16]{4,3,2,1,0:T(8,128)}, u32[]{:S(2)}) copy-start(f32[2,5,2,8,16]{4,3,2,1,0:T(8,128)} %param.13) | copy-start | bytes 30724
  2.5 3.2 %collective-permute-start = (f32[64,128]{1,0:T(8,128)}, f32[64,128]{1,0:T(8,128)S(1)}, u32[]{:S(2)}, u32[]{:S(2)}) collective-permute-start(f32[64,128]{1,0:T(8,128)} %get-tuple-element.15), channel_id=1, source_target_pairs={{0,1},{1,0},{2,3},{3,2},{4,5},{5,4},{6,7},{7,6},{8,9},{9,8},{10,11... | collective-permute-start | bytes 98312 | tf_op jit(solution)/shard_map/ppermute | solution.py:466
  5.7 0.8 %copy-start.4 = (f32[64,128]{1,0:T(8,128)S(1)}, f32[64,128]{1,0:T(8,128)}, u32[]{:S(2)}) copy-start(f32[64,128]{1,0:T(8,128)} %get-tuple-element.14.own_ref) | copy-start | bytes 98308
  6.5 11.2 %collective-permute-start.1 = (f32[96,128]{1,0:T(8,128)S(1)}, f32[96,128]{1,0:T(8,128)S(1)}, u32[]{:S(2)}, u32[]{:S(2)}) collective-permute-start(f32[96,128]{1,0:T(8,128)S(1)} %get-tuple-element.17), channel_id=1, source_target_pairs={{0,2},{1,3},{2,0},{3,1},{4,6},{5,7},{6,4},{7,5},{8,10},{9,11},{10,... | collective-permute-start | bytes 147464 | tf_op jit(solution)/shard_map/ppermute | solution.py:488
  10.0 9.3 %collective-permute-start.2 = (f32[96,128]{1,0:T(8,128)S(1)}, f32[96,128]{1,0:T(8,128)S(1)}, u32[]{:S(2)}, u32[]{:S(2)}) collective-permute-start(f32[96,128]{1,0:T(8,128)S(1)} %get-tuple-element.18), channel_id=1, source_target_pairs={{4,66},{66,4},{5,67},{67,5},{8,70},{70,8},{9,71},{71,9},{12,74},{7... | collective-permute-start | bytes 147464 | tf_op jit(solution)/shard_map/ppermute | solution.py:487
  14.0 1.0 %copy-start.1 = (bf16[512,256]{1,0:T(8,128)(2,1)S(1)}, bf16[512,256]{1,0:T(8,128)(2,1)}, u32[]{:S(2)}) copy-start(bf16[512,256]{1,0:T(8,128)(2,1)} %merge_in.1) | copy-start | bytes 786436
  15.0 0.9 %copy-start.2 = (bf16[256,512]{1,0:T(8,128)(2,1)S(1)}, bf16[256,512]{1,0:T(8,128)(2,1)}, u32[]{:S(2)}) copy-start(bf16[256,512]{1,0:T(8,128)(2,1)} %expand_in.1) | copy-start | bytes 786436
  15.9 0.7 %copy-start.5 = (f32[7,256]{1,0:T(8,128)S(1)}, f32[7,256]{1,0:T(8,128)}, u32[]{:S(2)}) copy-start(f32[7,256]{1,0:T(8,128)} %embed_ref.1) | copy-start | bytes 21508
  16.6 0.7 %copy-start.6 = (bf16[128,5]{0,1:T(8,128)(2,1)S(1)}, bf16[128,5]{0,1:T(8,128)(2,1)}, u32[]{:S(2)}) copy-start(bf16[128,5]{0,1:T(8,128)(2,1)} %param.19) | copy-start | bytes 3844
